TPU v7x, 32 devices: a whole 2x2x4 slice. The times are simulated.
32 devices in a mesh: parts: 2 (over x), tensor: 16 (over z, y, core).
Axes of the slice: x: 2, y: 2, z: 4, core: 2. Of those that a mesh axis runs over, the one named last changes fastest.
Arguments:
- hidden: bfloat16 [1024, 28672], P('parts', 'tensor'), parts along dimension 0, may hold values from -6 to 6
- frozen_weight: bfloat16 [28672, 8192], P('tensor'), may hold values from -0.03125 to 0.03125
- adapter_input_maps: bfloat16 [64, 16, 28672], P(('parts', 'tensor')), parts along dimension 0, may hold values from -0.03125 to 0.03125
- adapter_output_maps: bfloat16 [64, 16, 8192], P(('parts', 'tensor')), parts along dimension 0, may hold values from -1.5 to 1.5
- adapter_per_block: int32 [128], P('parts'), parts along dimension 0, may hold values from 0 to 31, as said below
- rows_per_block: int32 [128], P('parts'), parts along dimension 0, may hold values from 1 to 8, as said below
- cotangent: bfloat16 [1024, 8192], P('parts', 'tensor'), parts along dimension 0, may hold values from -6 to 6
Outputs:
- output: bfloat16 [1024, 8192], P('parts', 'tensor'), parts along dimension 0
- hidden_gradient: bfloat16 [1024, 28672], P('parts', 'tensor'), parts along dimension 0
- input_map_gradient: float32 [64, 16, 28672], P(('parts', 'tensor')), parts along dimension 0
- output_map_gradient: float32 [64, 16, 8192], P(('parts', 'tensor')), parts along dimension 0
There are 2 independent parts, one for each index of `parts`. A program takes and returns all parts, laid end to end along the dimension named above; an argument that names none is the same for every part. Nothing has to cross between parts.
Inputs may be any that keep to these rules, and one draw needn't show every extreme that they name: `adapter_per_block`: adapter a is held by index a // 2 of tensor. The blocks that name adapters of one holder number at most 8, and exactly 8 for some holder. `rows_per_block`: some block is full.
All inputs are finite; a program needn't handle non-finite values.
Results may differ from a plain program's by a relative error of at most 0.0032.
Values may be sent and summed in bfloat16 or wider, within the bound.
A program may use at most 256 MiB of HBM per device.

v0:
```python
import jax
import jax.numpy as jnp
from jax import lax
from jax.sharding import PartitionSpec as P

adapter_scale = 0.5


def local(
    hidden,
    frozen_weight,
    adapter_input_maps,
    adapter_output_maps,
    adapter_per_block,
    rows_per_block,
    cotangent,
):
    members = lax.axis_size("tensor")
    my_index = lax.axis_index("tensor")
    tokens, ff_slab = hidden.shape
    blocks = adapter_per_block.shape[0]
    block_len = tokens // blocks
    resident_adapters, rank_width, hidden_total = adapter_input_maps.shape
    d_slab = cotangent.shape[1]
    capacity = max(2, 2 * blocks // members)
    live_mask = jnp.arange(block_len)[None, :] < rows_per_block[:, None]
    adapter_full = None
    owners_of = adapter_per_block // resident_adapters
    before = jnp.arange(blocks)[None, :] < jnp.arange(blocks)[:, None]
    rank_in = jnp.sum((owners_of[None, :] == owners_of[:, None]) & before, axis=1)
    slot_of = owners_of * capacity + rank_in
    placing = (jnp.arange(members * capacity)[:, None] == slot_of[None, :]).astype(jnp.float32)
    place_half = placing.astype(jnp.bfloat16)
    masked = jnp.where(live_mask[:, :, None], hidden.reshape(blocks, block_len, ff_slab), 0)
    outgoing = jnp.einsum(
        "sb,bkf->skf", place_half, masked, preferred_element_type=jnp.float32
    ).astype(jnp.bfloat16)
    arrived = lax.all_to_all(
        outgoing.reshape(members, capacity, block_len, ff_slab),
        "tensor",
        split_axis=0,
        concat_axis=0,
        tiled=True,
    )
    local_position = lax.dynamic_slice_in_dim(placing, my_index * capacity, capacity, 0)
    own_half = local_position.astype(jnp.bfloat16)
    local_hot = (
        (adapter_per_block - my_index * resident_adapters)[:, None]
        == jnp.arange(resident_adapters)[None, :]
    ).astype(jnp.float32)
    chooser = jnp.dot(local_position, local_hot, precision=lax.Precision.HIGHEST)
    selector_half = chooser.astype(jnp.bfloat16)
    slot_a = jnp.einsum(
        "py,ybg->pbg", selector_half, adapter_input_maps, preferred_element_type=jnp.float32
    ).astype(jnp.bfloat16)
    slot_b = jnp.einsum(
        "oy,ysi->osi", selector_half, adapter_output_maps, preferred_element_type=jnp.float32
    ).astype(jnp.bfloat16)
    slot_a_split = slot_a.reshape(capacity, rank_width, members, ff_slab)
    slot_b_split = slot_b.reshape(capacity, rank_width, members, d_slab)
    low_rank = jnp.einsum(
        "mckf,crmf->ckr", arrived, slot_a_split, preferred_element_type=jnp.float32
    ).astype(jnp.bfloat16)
    adapter_output = adapter_scale * jnp.einsum(
        "ckr,crmd->mckd", low_rank, slot_b_split, preferred_element_type=jnp.float32
    )
    own_live = jnp.dot(
        local_position, live_mask.astype(jnp.float32), precision=lax.Precision.HIGHEST
    )
    dispersed = jnp.einsum(
        "co,mckd->mokd", local_position, adapter_output, precision=lax.Precision.HIGHEST
    )
    adapter_full = dispersed.reshape(members, tokens, d_slab)
    weight_split = frozen_weight.reshape(ff_slab, members, d_slab)
    summand = jnp.einsum("tf,fmd->mtd", hidden, weight_split, preferred_element_type=jnp.float32)
    summand = summand + adapter_full
    summed = lax.psum_scatter(summand, "tensor", scatter_dimension=0, tiled=True)[0]
    output = summed.astype(jnp.bfloat16)
    shard_part = lax.all_gather(cotangent, "tensor", axis=1, tiled=True)
    columns = shard_part.shape[1]
    frozen_gradient = jnp.einsum(
        "tc,fc->tf", shard_part, frozen_weight, preferred_element_type=jnp.float32
    )
    own_dy = jnp.einsum(
        "gt,tni->gni",
        own_half,
        shard_part.reshape(blocks, block_len, columns),
        preferred_element_type=jnp.float32,
    ).astype(jnp.bfloat16)
    back_low = jnp.einsum("ckd,crd->ckr", own_dy, slot_b, preferred_element_type=jnp.float32)
    per_slot = jnp.einsum("ckr,ckd->crd", low_rank, own_dy, preferred_element_type=jnp.float32)
    per_adapter = jnp.einsum("ca,crd->ard", chooser, per_slot, precision=lax.Precision.HIGHEST)
    column_gradients = per_adapter
    folded = (frozen_gradient, back_low, column_gradients)
    frozen_gradient, back_low, column_gradients = folded
    back_half = (back_low * own_live[:, :, None]).astype(jnp.bfloat16)
    output_map_gradient = adapter_scale * column_gradients
    per_slot_a = jnp.einsum(
        "ckr,mckf->crmf", back_half, arrived, preferred_element_type=jnp.float32
    ).reshape(capacity, rank_width, hidden_total)
    input_map_gradient = adapter_scale * jnp.einsum(
        "ca,crf->arf", chooser, per_slot_a, precision=lax.Precision.HIGHEST
    )
    adapter_gradient = (
        adapter_scale
        * jnp.einsum("ckr,crmf->mckf", back_half, slot_a_split, preferred_element_type=jnp.float32)
    ).astype(jnp.bfloat16)
    returned_rows = lax.all_to_all(
        adapter_gradient, "tensor", split_axis=0, concat_axis=0, tiled=True
    )
    adapter_rows = jnp.einsum(
        "sb,skf->bkf",
        place_half,
        returned_rows.reshape(members * capacity, block_len, ff_slab),
        preferred_element_type=jnp.float32,
    ).reshape(tokens, ff_slab)
    hidden_gradient = (frozen_gradient + adapter_rows).astype(jnp.bfloat16)
    return (output, hidden_gradient, input_map_gradient, output_map_gradient)


def solution(mesh):
    in_specs = (
        P("parts", "tensor"),
        P("tensor", None),
        P(("parts", "tensor"), None, None),
        P(("parts", "tensor"), None, None),
        P("parts"),
        P("parts"),
        P("parts", "tensor"),
    )
    out_specs = (
        P("parts", "tensor"),
        P("parts", "tensor"),
        P(("parts", "tensor"), None, None),
        P(("parts", "tensor"), None, None),
    )
    return jax.shard_map(local, mesh=mesh, in_specs=in_specs, out_specs=out_specs, check_vma=False)
```

profile of v0, /device:TPU:0, one launch (start us, length us, event | category | flops | bytes accessed | tf_op | source)
XLA Modules:
  0.0 492.7 jit_solution(220811324084626573)
XLA Ops:
  7.2 0.0 copy-start
  7.2 0.0 all-gather.2.cloned.1.call-start
  7.2 0.7 all-gather.2.cloned.1.call-update
  7.9 0.7 and_select_fusion
  8.6 0.2 convert_reduce_fusion
  8.8 0.7 iota_compare_fusion.4
  9.4 2.7 fusion.13
  12.1 3.8 copy.81
  16.0 7.4 %all-to-all-start = ((bf16[16,8,8,1792]{3,2,1,0:T(8,128)(2,1)}), bf16[16,8,8,1792]{3,2,1,0:T(8,128)(2,1)}, u32[]{:S(2)}, u32[]{:S(2)}) async-start(bf16[16,8,8,1792]{3,2,1,0:T(8,128)(2,1)} %copy.81), calls=%async_computation | async-start | bytes 7340032 | tf_op jit(solution)/shard_map/all_to_all | solution.py:38
  23.4 0.0 reduce-scatter.2.cloned.1.call-start
  23.4 0.0 copy-start.5
  23.5 36.1 %copy.109 = bf16[1792,8192]{0,1:T(8,128)(2,1)} copy(bf16[1792,8192]{1,0:T(8,128)(2,1)} %param.8) | data formatting | bytes 58720256 | tf_op jit(solution)/shard_map/reshape | solution.py:74
  59.6 0.2 fusion.50
  59.9 0.0 copy-done.5
  59.9 2.0 convolution_convert_fusion.1
  61.9 0.0 copy-done
  61.9 5.6 %convolution_convert_fusion = bf16[8,16,28672]{2,0,1:T(8,128)(2,1)} fusion(bf16[2,16,28672]{2,1,0:T(8,128)(2,1)S(1)} %copy-done, f32[8,2]{0,1:T(2,128)S(1)} %fusion.50), kind=kOutput, calls=%fused_computation | convolution fusion | flops 18350096 | bytes 9175104 | tf_op jit(solution)/shard_map/py,ybg->pbg/dot_general | solution.py:53
  67.5 61.0 %all-to-all-done = bf16[16,8,8,1792]{3,2,1,0:T(8,128)(2,1)} async-done(((bf16[16,8,8,1792]{3,2,1,0:T(8,128)(2,1)}), bf16[16,8,8,1792]{3,2,1,0:T(8,128)(2,1)}, u32[]{:S(2)}, u32[]{:S(2)}) %all-to-all-start) | async-done | bytes 3670048 | tf_op jit(solution)/shard_map/all_to_all | solution.py:38
  128.5 0.0 copy-start.2
  128.5 8.4 %fusion.33 = bf16[8,8,16]{2,1,0:T(8,128)(2,1)S(1)} fusion(bf16[16,8,8,1792]{3,2,1,0:T(8,128)(2,1)} %all-to-all-done, bf16[8,16,16,1792]{3,0,2,1:T(8,128)(2,1)} %bitcast.79), kind=kOutput, calls=%fused_computation.36 | convolution fusion | flops 58721280 | bytes 11012096 | tf_op jit(solution)/shard_map/mckf,crmf->ckr/dot_general | solution.py:61
  136.9 0.0 copy-done.2
  136.9 2.4 multiply_bitcast_fusion
  139.2 8.2 %convolution_bitcast_fusion = f32[16,64,8,512]{3,1,2,0:T(8,128)S(1)} fusion(f32[16,8,8,512]{3,2,0,1:T(8,128)S(1)} %multiply_bitcast_fusion, pred[128,64]{1,0:T(8,128)(4,1)S(1)} %get-tuple-element.21, s32[]{:T(128)S(6)} %select_n.13), kind=kOutput, calls=%fused_computation.7 | convolution fusion | flops 402653184 | bytes 18875396 | tf_op jit(solution)/shard_map/co,mckd->mokd/dot_general | solution.py:70
  147.4 11.8 %copy.160 = f32[16,64,8,512]{3,2,1,0:T(8,128)} copy(f32[16,64,8,512]{3,1,2,0:T(8,128)S(1)} %convolution_bitcast_fusion) | data formatting | bytes 33554432 | tf_op jit(solution)/shard_map/co,mckd->mokd/transpose | solution.py:70
  159.2 0.0 copy-start.4
  159.2 17.7 %copy.87 = f32[16,512,512]{1,2,0:T(8,128)} copy(f32[16,512,512]{2,1,0:T(8,128)} %bitcast.77) | data formatting | bytes 33554432 | tf_op jit(solution)/shard_map/reshape | solution.py:73
  176.9 0.0 copy-done.4
  176.9 28.0 %bitcast_add_fusion = f32[16,512,512]{1,2,0:T(8,128)} fusion(f32[16,512,512]{1,2,0:T(8,128)} %copy.87, bf16[1792,16,512]{0,2,1:T(8,128)(2,1)} %bitcast.78, bf16[512,1792]{1,0:T(8,128)(2,1)S(1)} %copy-done.4), kind=kOutput, calls=%fused_computation.2 | convolution fusion | flops 15036579840 | bytes 64749568 | tf_op jit(solution)/shard_map/tf,fmd->mtd/dot_general | solution.py:75
  204.9 0.0 copy-start.6
  204.9 0.0 reduce-scatter.2.cloned.1.call-update
  204.9 0.6 copy-done.6
  205.5 0.1 fusion.64
  205.7 0.0 all-gather.2.cloned.1.call-done
  205.7 0.0 copy-start.3
  205.7 12.4 %convolution_convert_fusion.2 = bf16[8,8,8192]{2,0,1:T(8,128)(2,1)S(1)} fusion(bf16[64,8,8192]{2,1,0:T(8,128)(2,1)} %bitcast.81, bf16[128,64]{1,0:T(8,128)(2,1)S(1)} %get-tuple-element.20, s32[]{:T(128)S(6)} %select_n.13), kind=kOutput, calls=%fused_computation.5 | convolution fusion | flops 67633152 | bytes 9439236 | tf_op jit(solution)/shard_map/gt,tni->gni/dot_general | solution.py:84
  218.0 0.0 copy-done.3
  218.0 1.7 fusion.39
  219.7 11.3 %fusion.14 = bf16[16,8,8,1792]{3,2,0,1:T(8,128)(2,1)S(1)} fusion(bf16[8,8,16,1]{2,1,3,0:T(8,128)(2,1)S(1)} %fusion.39, bf16[8,16,16,1792]{3,0,2,1:T(8,128)(2,1)} %bitcast.80), kind=kOutput, calls=%fused_computation.23 | convolution fusion | flops 62390272 | bytes 11012096 | tf_op jit(solution)/shard_map/ckr,crmf->mckf/dot_general | solution.py:106
  231.1 2.2 copy.92
  233.3 30.4 %all-to-all-start.1 = ((bf16[16,8,8,1792]{3,2,1,0:T(8,128)(2,1)}), bf16[16,8,8,1792]{3,2,1,0:T(8,128)(2,1)}, u32[]{:S(2)}, u32[]{:S(2)}) async-start(bf16[16,8,8,1792]{3,2,1,0:T(8,128)(2,1)} %copy.92), calls=%async_computation.2 | async-start | bytes 7340032 | tf_op jit(solution)/shard_map/all_to_all | solution.py:108
  263.7 1.3 fusion.42
  265.0 5.8 %convolution_multiply_fusion.1 = f32[2,16,8192]{2,0,1:T(2,128)S(1)} fusion(f32[8,16,8192]{2,1,0:T(8,128)S(1)} %fusion.42, f32[8,2]{0,1:T(2,128)S(1)} %fusion.50), kind=kOutput, calls=%fused_computation.6 | convolution fusion | flops 25427968 | bytes 5242944 | tf_op jit(solution)/shard_map/ca,crd->ard/dot_general | solution.py:92
  270.9 1.6 copy.103
  272.5 8.0 %fusion.9 = f32[8,16,16,1792]{3,1,2,0:T(8,128)} fusion(bf16[8,8,16,1]{2,1,3,0:T(8,128)(2,1)S(1)} %fusion.39, bf16[16,8,8,1792]{3,2,1,0:T(8,128)(2,1)} %all-to-all-done), kind=kOutput, calls=%fused_computation.18 | convolution fusion | flops 58720256 | bytes 18352128 | tf_op jit(solution)/shard_map/ckr,mckf->crmf/dot_general | solution.py:98
  280.5 18.8 %copy.112 = f32[8,16,16,1792]{3,2,0,1:T(8,128)} copy(f32[8,16,16,1792]{3,1,2,0:T(8,128)} %fusion.9) | data formatting | bytes 29360128 | tf_op jit(solution)/shard_map/reshape | solution.py:100
  299.3 13.3 %reshape.85 = f32[8,16,28672]{2,0,1:T(8,128)} reshape(f32[8,16,16,1792]{3,2,0,1:T(8,128)} %copy.112) | data formatting | bytes 29360128 | tf_op jit(solution)/shard_map/reshape | solution.py:100
  312.7 17.1 %convolution_multiply_fusion = f32[2,16,28672]{2,0,1:T(2,128)S(1)} fusion(f32[8,16,28672]{2,0,1:T(8,128)} %reshape.85, f32[8,2]{0,1:T(2,128)S(1)} %fusion.50), kind=kOutput, calls=%fused_computation.1 | convolution fusion | flops 88997888 | bytes 18350144 | tf_op jit(solution)/shard_map/ca,crf->arf/dot_general | solution.py:101
  329.8 4.0 copy.102
  333.7 48.5 %all-to-all-done.1 = bf16[16,8,8,1792]{3,2,1,0:T(8,128)(2,1)} async-done(((bf16[16,8,8,1792]{3,2,1,0:T(8,128)(2,1)}), bf16[16,8,8,1792]{3,2,1,0:T(8,128)(2,1)}, u32[]{:S(2)}, u32[]{:S(2)}) %all-to-all-start.1) | async-done | bytes 3670048 | tf_op jit(solution)/shard_map/all_to_all | solution.py:108
  382.2 5.4 %fusion.11 = f32[64,8,1792]{2,0,1:T(8,128)} fusion(bf16[128,8,1792]{2,1,0:T(8,128)(2,1)} %bitcast.24, s32[64]{0:T(128)S(1)} %multiply_add_fusion), kind=kOutput, calls=%fused_computation.20 | convolution fusion | flops 234905600 | bytes 7340288 | tf_op jit(solution)/shard_map/sb,skf->bkf/dot_general | solution.py:111
  387.6 0.0 copy-start.1
  387.6 25.6 %fusion.8 = bf16[512,1792]{1,0:T(8,128)(2,1)} fusion(f32[64,8,1792]{2,0,1:T(8,128)} %fusion.11, bf16[512,8192]{1,0:T(8,128)(2,1)} %all-gather.2.cloned.1.call-done, bf16[1792,8192]{1,0:T(8,128)(2,1)} %param.8), kind=kOutput, calls=%fused_computation.17 | convolution fusion | flops 15034220544 | bytes 43253760 | tf_op jit(solution)/shard_map/tc,fc->tf/dot_general | solution.py:81
  413.2 70.1 %reduce-scatter.2.cloned.1.call-done = f32[1,512,512]{1,2,0:T(8,128)} async-done(((f32[16,512,512]{1,2,0:T(8,128)}), f32[1,512,512]{1,2,0:T(8,128)}) %reduce-scatter.2.cloned.1.call-update) | async-done | bytes 1048592 | tf_op jit(solution)/shard_map/reduce_scatter | solution.py:77
  483.4 1.3 convert_bitcast_fusion
  484.7 1.0 copy.101
  485.7 0.0 copy-done.1
  (2 shorter events, 0.0 us)
Async XLA Ops:
  7.2 54.7 %copy-start = (bf16[2,16,28672]{2,1,0:T(8,128)(2,1)S(1)}, bf16[2,16,28672]{2,1,0:T(8,128)(2,1)}, u32[]{:S(2)}) copy-start(bf16[2,16,28672]{2,1,0:T(8,128)(2,1)} %param.9) | copy-start | bytes 5505028
  7.2 198.5 %all-gather.2.cloned.1.call-start = ((), (), s32[]{:S(2)}) async-start(), calls=%async_computation.4 | async-start | bytes 8912896 | tf_op jit(solution)/shard_map/all_gather | solution.py:79
  16.0 112.5 %all-to-all-start = ((bf16[16,8,8,1792]{3,2,1,0:T(8,128)(2,1)}), bf16[16,8,8,1792]{3,2,1,0:T(8,128)(2,1)}, u32[]{:S(2)}, u32[]{:S(2)}) async-start(bf16[16,8,8,1792]{3,2,1,0:T(8,128)(2,1)} %copy.81), calls=%async_computation | async-start | bytes 7340032 | tf_op jit(solution)/shard_map/all_to_all | solution.py:38
  23.4 460.0 %reduce-scatter.2.cloned.1.call-start = ((), (), s32[]{:S(2)}) async-start(), calls=%async_computation.3 | async-start | bytes 17825792 | tf_op jit(solution)/shard_map/reduce_scatter | solution.py:77
  23.4 36.4 %copy-start.5 = (bf16[2,16,8192]{2,1,0:T(8,128)(2,1)S(1)}, bf16[2,16,8192]{2,1,0:T(8,128)(2,1)}, u32[]{:S(2)}) copy-start(bf16[2,16,8192]{2,1,0:T(8,128)(2,1)} %param.10) | copy-start | bytes 1572868
  128.5 8.4 %copy-start.2 = (bf16[8,16,8192]{2,0,1:T(8,128)(2,1)S(1)}, bf16[8,16,8192]{2,0,1:T(8,128)(2,1)}, u32[]{:S(2)}) copy-start(bf16[8,16,8192]{2,0,1:T(8,128)(2,1)} %convolution_convert_fusion.1) | copy-start | bytes 6291460
  159.2 17.7 %copy-start.4 = (bf16[512,1792]{1,0:T(8,128)(2,1)S(1)}, bf16[512,1792]{1,0:T(8,128)(2,1)}, u32[]{:S(2)}) copy-start(bf16[512,1792]{1,0:T(8,128)(2,1)} %param.7) | copy-start | bytes 5505028
  204.9 0.7 copy-start.6
  205.7 12.4 %copy-start.3 = (bf16[8,16,8192]{2,0,1:T(8,128)(2,1)S(1)}, bf16[8,16,8192]{2,0,1:T(8,128)(2,1)}, u32[]{:S(2)}) copy-start(bf16[8,16,8192]{2,0,1:T(8,128)(2,1)} %convolution_convert_fusion.1) | copy-start | bytes 6291460
  233.3 148.9 %all-to-all-start.1 = ((bf16[16,8,8,1792]{3,2,1,0:T(8,128)(2,1)}), bf16[16,8,8,1792]{3,2,1,0:T(8,128)(2,1)}, u32[]{:S(2)}, u32[]{:S(2)}) async-start(bf16[16,8,8,1792]{3,2,1,0:T(8,128)(2,1)} %copy.92), calls=%async_computation.2 | async-start | bytes 7340032 | tf_op jit(solution)/shard_map/all_to_all | solution.py:108
  387.6 98.1 %copy-start.1 = (bf16[2,16,28672]{2,1,0:T(8,128)(2,1)S(1)}, bf16[2,16,28672]{2,1,0:T(8,128)(2,1)}, u32[]{:S(2)}) copy-start(bf16[2,16,28672]{2,1,0:T(8,128)(2,1)} %param.9) | copy-start | bytes 5505028
Sparse Core Ops, SparseCore 0:
  10.2 147.4 all-gather.1
  205.0 278.2 reduce-scatter.1
where the time goes:
time: 499 us; the launch traced here: 493 us
  waiting for transfers between devices  180 us (36%)
  matrix products  146 us (29%)
  local copies, waits for them, and re-layouts  111 us (22%)
  starting transfers between devices  37.9 us (8%)
  between operations  14.4 us (3%)
    reduce_scatter x1, waiting for transfers between devices, local(): lax.psum_scatter(summand, 'tensor', scatter_dimension=0, tiled=True)[0]  70.1 us
    all_to_all x1, waiting for transfers between devices, local(): lax.all_to_all(outgoing.reshape(members, capacity, block_len, ff_slab), '...  61 us
    all_to_all x1, waiting for transfers between devices, local(): lax.all_to_all(adapter_gradient, 'tensor', split_axis=0, concat_axis=0, t...  48.5 us
    reshape x1, local copies, waits for them, and re-layouts, local(): weight_split = frozen_weight.reshape(ff_slab, members, d_slab)  36.1 us
    reshape x2, local copies, waits for them, and re-layouts, local(): per_slot_a = jnp.einsum('ckr,mckf->crmf', back_half, arrived, preferred_e...  32.1 us
    all_to_all x1, starting transfers between devices, local(): lax.all_to_all(adapter_gradient, 'tensor', split_axis=0, concat_axis=0, t...  30.4 us
    dot_general x1, matrix products, local(): jnp.einsum('tf,fmd->mtd', hidden, weight_split, preferred_element_type=jn...  28 us
    dot_general x1, matrix products, local(): jnp.einsum('tc,fc->tf', shard_part, frozen_weight, preferred_element_type...  25.6 us
  transfers between devices with their start and end apart: 4, of which 3 were waited for; matrix products, arithmetic and copies ran while one was open for 52% of the time, Pallas kernels for 0%

commit v1 on v0

v1 whole, which is shorter than its diff:
```python
import functools

import jax
import jax.numpy as jnp
from jax import lax
from jax.experimental import pallas as pl
from jax.experimental.pallas import tpu as pltpu
from jax.sharding import PartitionSpec as P

adapter_scale = 0.5
vmem_bytes = 32 * 1024 * 1024
narrow_bits = (2, 8)


def partners(members, bit):
    return [(i, i ^ bit) for i in range(members)]


def swap(value, members, bit):
    return lax.ppermute(value, "tensor", partners(members, bit))


def forward_kernel(places, hidden_ref, weight_ref, *rest):
    out_ref = rest[-1]
    out_ref[0] = jnp.dot(hidden_ref[...], weight_ref[...], preferred_element_type=jnp.float32)


def forward_slabs(places, hidden, weight, width, earlier=()):
    tokens, depth = hidden.shape
    count = places.shape[0]
    return pl.pallas_call(
        forward_kernel,
        grid_spec=pltpu.PrefetchScalarGridSpec(
            num_scalar_prefetch=1,
            grid=(count,),
            in_specs=[
                pl.BlockSpec((tokens, depth), lambda j, places: (0, 0)),
                pl.BlockSpec((depth, width), lambda j, places: (0, places[j])),
            ]
            + [pl.BlockSpec(memory_space=pl.ANY)] * len(earlier),
            out_specs=pl.BlockSpec((1, tokens, width), lambda j, places: (j, 0, 0)),
        ),
        out_shape=jax.ShapeDtypeStruct((count, tokens, width), jnp.float32),
        compiler_params=pltpu.CompilerParams(vmem_limit_bytes=vmem_bytes),
        cost_estimate=pl.CostEstimate(
            flops=2 * count * tokens * depth * width,
            bytes_accessed=count * width * (2 * depth + 4 * tokens),
            transcendentals=0,
        ),
        name="forward_slabs",
    )(places, hidden, weight, *earlier)


def gradient_kernel(steps, places, slab_ref, first_ref, second_ref, start_ref, *rest):
    out_ref, total = rest[-2:]
    step = pl.program_id(0)
    across = (((1,), (1,)), ((), ()))
    term = lax.dot_general(
        slab_ref[0], first_ref[...], across, preferred_element_type=jnp.float32
    ) + lax.dot_general(slab_ref[1], second_ref[...], across, preferred_element_type=jnp.float32)

    @pl.when(step == 0)
    def _():
        total[...] = start_ref[...].astype(jnp.float32) + term

    @pl.when(step > 0)
    def _():
        total[...] += term

    @pl.when(step == steps - 1)
    def _():
        out_ref[...] = total[...].astype(out_ref.dtype)


def add_gradient(places, slabs, weight, start, dtype, earlier=()):
    count, tokens, width = slabs.shape
    depth = weight.shape[0]
    steps = count // 2
    return pl.pallas_call(
        functools.partial(gradient_kernel, steps),
        grid_spec=pltpu.PrefetchScalarGridSpec(
            num_scalar_prefetch=1,
            grid=(steps,),
            in_specs=[
                pl.BlockSpec((2, tokens, width), lambda j, places: (j, 0, 0)),
                pl.BlockSpec((depth, width), lambda j, places: (0, places[2 * j])),
                pl.BlockSpec((depth, width), lambda j, places: (0, places[2 * j + 1])),
                pl.BlockSpec((tokens, depth), lambda j, places: (0, 0)),
            ]
            + [pl.BlockSpec(memory_space=pl.ANY)] * len(earlier),
            out_specs=pl.BlockSpec((tokens, depth), lambda j, places: (0, 0)),
            scratch_shapes=[pltpu.VMEM((tokens, depth), jnp.float32)],
        ),
        out_shape=jax.ShapeDtypeStruct((tokens, depth), dtype),
        compiler_params=pltpu.CompilerParams(vmem_limit_bytes=vmem_bytes),
        cost_estimate=pl.CostEstimate(
            flops=2 * count * tokens * depth * width,
            bytes_accessed=2 * count * width * (depth + tokens),
            transcendentals=0,
        ),
        name="hidden_gradient",
    )(places, slabs, weight, weight, start, *earlier)


def whole_call(kernel, ins, out_shapes, earlier, name):
    return pl.pallas_call(
        kernel,
        in_specs=[pl.BlockSpec(memory_space=pltpu.VMEM)] * len(ins)
        + [pl.BlockSpec(memory_space=pl.ANY)] * len(earlier),
        out_specs=pl.BlockSpec(memory_space=pltpu.VMEM),
        out_shape=out_shapes,
        compiler_params=pltpu.CompilerParams(vmem_limit_bytes=vmem_bytes),
        name=name,
    )(*ins, *earlier)


def join_kernel(mine_ref, other_ref, *rest):
    rest[-1][...] = mine_ref[...] + other_ref[...].astype(jnp.float32)


def join(mine, other, earlier):
    shape = jax.ShapeDtypeStruct(mine.shape, jnp.float32)
    return whole_call(join_kernel, (mine, other), shape, earlier, "join")


def place_kernel(ff_slab, grads_ref, *rest):
    in_ref, out_ref = rest[-2:]
    grads = grads_ref[0].astype(jnp.float32)
    in_ref[...] = grads[:, :ff_slab].reshape(in_ref.shape)
    out_ref[...] = grads[:, ff_slab:].reshape(out_ref.shape)


def place_gradients(grads, resident, ff_slab, earlier):
    members, held_rows, width = grads.shape
    rank_width = held_rows // resident
    d_slab = width - ff_slab
    return pl.pallas_call(
        functools.partial(place_kernel, ff_slab),
        grid=(members,),
        in_specs=[pl.BlockSpec((1, held_rows, width), lambda m: (m, 0, 0))]
        + [pl.BlockSpec(memory_space=pl.ANY)] * len(earlier),
        out_specs=[
            pl.BlockSpec((resident, rank_width, ff_slab), lambda m: (0, 0, m)),
            pl.BlockSpec((resident, rank_width, d_slab), lambda m: (0, 0, m)),
        ],
        out_shape=[
            jax.ShapeDtypeStruct((resident, rank_width, members * ff_slab), jnp.float32),
            jax.ShapeDtypeStruct((resident, rank_width, members * d_slab), jnp.float32),
        ],
        compiler_params=pltpu.CompilerParams(vmem_limit_bytes=vmem_bytes),
        name="place_gradients",
    )(grads, *earlier)


def pair_kernel(ff_slab, maps_ref, hidden_ref, cotangent_ref, picker_ref, *rest):
    out_ref = rest[-1]
    adapters, _, tokens = picker_ref.shape
    rank_width = maps_ref.shape[0] // adapters
    across = (((1,), (1,)), ((), ()))
    low = lax.dot_general(
        maps_ref[:, :ff_slab], hidden_ref[...], across, preferred_element_type=jnp.float32
    )
    back = lax.dot_general(
        maps_ref[:, ff_slab:], cotangent_ref[...], across, preferred_element_type=jnp.float32
    )
    by_rank = (adapters, rank_width, tokens)
    out_ref[:rank_width] = jnp.sum(low.reshape(by_rank) * picker_ref[...], axis=0)
    out_ref[rank_width:] = jnp.sum(back.reshape(by_rank) * picker_ref[...], axis=0)


def low_rank_pair(maps, hidden, cotangent, picker, earlier):
    adapters, _, tokens = picker.shape
    rank_width = maps.shape[0] // adapters
    return pl.pallas_call(
        functools.partial(pair_kernel, hidden.shape[1]),
        in_specs=[pl.BlockSpec(memory_space=pltpu.VMEM)] * 4
        + [pl.BlockSpec(memory_space=pl.ANY)] * len(earlier),
        out_specs=pl.BlockSpec(memory_space=pltpu.VMEM),
        out_shape=jax.ShapeDtypeStruct((2 * rank_width, tokens), jnp.float32),
        compiler_params=pltpu.CompilerParams(vmem_limit_bytes=vmem_bytes),
        cost_estimate=pl.CostEstimate(
            flops=2 * maps.size * tokens,
            bytes_accessed=2 * (maps.size + hidden.size + cotangent.size),
            transcendentals=0,
        ),
        name="low_rank_pair",
    )(maps, hidden, cotangent, picker, *earlier)


def local(
    hidden,
    frozen_weight,
    adapter_input_maps,
    adapter_output_maps,
    adapter_per_block,
    rows_per_block,
    cotangent,
):
    members = lax.axis_size("tensor")
    me = lax.axis_index("tensor")
    tokens, ff_slab = hidden.shape
    d_slab = cotangent.shape[1]
    blocks = adapter_per_block.shape[0]
    block_len = tokens // blocks
    resident, rank_width, hidden_total = adapter_input_maps.shape
    adapters = resident * members
    held_rows = resident * rank_width
    bits = [1 << i for i in range(members.bit_length() - 1)]

    split_in = adapter_input_maps.reshape(held_rows, members, ff_slab).transpose(1, 0, 2)
    split_out = adapter_output_maps.reshape(held_rows, members, d_slab).transpose(1, 0, 2)
    packed = jnp.concatenate([split_in, split_out], axis=2)
    maps = lax.all_to_all(packed, "tensor", 0, 0, tiled=True).reshape(
        members * held_rows, ff_slab + d_slab
    )
    maps_in, maps_out = maps[:, :ff_slab], maps[:, ff_slab:]

    slabs = lax.all_gather(cotangent, "tensor", axis=0)

    def send(value, bit):
        wire = jnp.bfloat16 if bit in narrow_bits else jnp.float32
        return swap(value.astype(wire), members, bit)

    half = members // 2
    sums = {}
    groups = []
    earlier = (packed,)
    for first in (half, 0):
        offsets = list(range(first + half - 1, first - 1, -1))
        group = forward_slabs(
            jnp.bitwise_xor(me, jnp.array(offsets, jnp.int32)),
            hidden,
            frozen_weight,
            d_slab,
            earlier,
        )
        groups.append(group)
        part = {k: group[j] for j, k in enumerate(offsets)}
        for k in offsets[1::2]:
            sums[k] = part[k] + send(part[k ^ 1], 1)
        earlier = ()

    for bit in bits[1:-1]:
        for k in [k for k in sums if k % (2 * bit) == bit]:
            if k >= half or bit == bits[1]:
                sums[k ^ bit] = join(sums[k ^ bit], send(sums[k], bit), groups[1:])
    ready = (sums[half],) + tuple(
        sums[k] for k in sums if k < half and k % (2 * bits[1]) == 0
    )

    live = (jnp.arange(block_len)[None, :] < rows_per_block[:, None]).reshape(tokens)
    row_adapter = jnp.broadcast_to(adapter_per_block[:, None], (blocks, block_len)).reshape(tokens)
    picker = (
        (jnp.arange(adapters)[:, None] == row_adapter[None, :]) & live[None, :]
    ).astype(jnp.float32)[:, None, :]
    pair = low_rank_pair(maps, hidden, cotangent, picker, ready)
    for bit in bits:
        pair = pair + swap(pair, members, bit)
    pair = pair.astype(jnp.bfloat16).astype(jnp.float32)
    flat = (adapters * rank_width, tokens)
    low_spread = (picker * pair[None, :rank_width]).astype(jnp.bfloat16).reshape(flat)
    back_spread = (picker * pair[None, rank_width:]).astype(jnp.bfloat16).reshape(flat)

    grad_in = adapter_scale * jnp.dot(back_spread, hidden, preferred_element_type=jnp.float32)
    grad_out = adapter_scale * jnp.dot(low_spread, cotangent, preferred_element_type=jnp.float32)
    grads = jnp.concatenate(
        [grad_in.astype(jnp.bfloat16), grad_out.astype(jnp.bfloat16)], axis=1
    ).reshape(members, held_rows, ff_slab + d_slab)
    sent = (grads,)
    grads = lax.all_to_all(grads, "tensor", 0, 0, tiled=True)

    down = (((0,), (0,)), ((), ()))
    lora_rows = (
        adapter_scale
        * lax.dot_general(back_spread, maps_in, down, preferred_element_type=jnp.float32)
    ).astype(jnp.bfloat16)
    hidden_gradient = add_gradient(
        jnp.arange(members, dtype=jnp.int32), slabs, frozen_weight, lora_rows, jnp.bfloat16, sent
    )

    for bit in bits[2:-1]:
        for k in [k for k in sums if k < half and k % (2 * bit) == bit]:
            sums[k ^ bit] = join(sums[k ^ bit], send(sums[k], bit), (hidden_gradient,))
    output_sum = join(sums[0], send(sums[half], half), (hidden_gradient,))
    input_map_gradient, output_map_gradient = place_gradients(
        grads, resident, ff_slab, (hidden_gradient,)
    )
    adapter_output = adapter_scale * lax.dot_general(
        low_spread, maps_out, down, preferred_element_type=jnp.float32
    )
    output = (output_sum + adapter_output).astype(jnp.bfloat16)
    return (output, hidden_gradient, input_map_gradient, output_map_gradient)


def solution(mesh):
    in_specs = (
        P("parts", "tensor"),
        P("tensor", None),
        P(("parts", "tensor"), None, None),
        P(("parts", "tensor"), None, None),
        P("parts"),
        P("parts"),
        P("parts", "tensor"),
    )
    out_specs = (
        P("parts", "tensor"),
        P("parts", "tensor"),
        P(("parts", "tensor"), None, None),
        P(("parts", "tensor"), None, None),
    )
    return jax.shard_map(local, mesh=mesh, in_specs=in_specs, out_specs=out_specs, check_vma=False)
```

time: 499 us -> 270 us (0.54); the launches traced: 493 us -> 269 us
  matrix products: 146 us -> 6.73 us
  local copies, waits for them, and re-layouts: 111 us -> 19 us
  Pallas kernels: 0 us -> 68.2 us
  waiting for transfers between devices: 180 us -> 122 us
  starting transfers between devices: 37.9 us -> 26.9 us
  other arithmetic: 2.83 us -> 11.9 us
    dot_general x18 -> x4, matrix products: 146 us -> 6.73 us  [the longest x1 2.64 us: local(): lax.dot_general(back_spread, maps_in, down, preferred_element_type=jnp.fl...]
    ppermute x0 -> x19, waiting for transfers between devices: none -> 121 us  [swap(): return lax.ppermute(value, 'tensor', partners(members, bit))]
    all_to_all x2, waiting for transfers between devices: 109 us -> 0.01 us  [the longest x1 0.01 us: local(): lax.all_to_all(packed, 'tensor', 0, 0, tiled=True)]
    reshape x5 -> x2, local copies, waits for them, and re-layouts: 89.8 us -> 0.83 us  [the longest x1 0.54 us: local(): adapter_input_maps.reshape(held_rows, members, ff_slab).transpose(1, 0, 2)]
    reduce_scatter x1 -> x0, waiting for transfers between devices: 70.1 us -> none  [local(): lax.psum_scatter(summand, 'tensor', scatter_dimension=0, tiled=True)[0]]
    pallas_call x0 -> x12, Pallas kernels: none -> 68.2 us  [the longest x2 24.9 us: forward_slabs(): pl.pallas_call(forward_kernel, grid_spec=pltpu.PrefetchScalarGridSpec(num...]
    all_to_all x2, starting transfers between devices: 37.8 us -> 12.3 us  [the longest x1 7.56 us: local(): lax.all_to_all(packed, 'tensor', 0, 0, tiled=True)]
    ppermute x0 -> x19, starting transfers between devices: none -> 14.6 us  [swap(): return lax.ppermute(value, 'tensor', partners(members, bit))]
  transfers between devices with their start and end apart: 4 -> 22, of which waited for: 3 -> 9; matrix products, arithmetic and copies ran while one was open for 52% -> 8% of each run, Pallas kernels for 0% -> 22%
where the time goes in v1:
time: 270 us; the launch traced here: 269 us
  waiting for transfers between devices  122 us (45%)
  Pallas kernels  68.2 us (25%)
  starting transfers between devices  26.9 us (10%)
  local copies, waits for them, and re-layouts  19 us (7%)
  between operations  14.4 us (5%)
  other arithmetic  11.9 us (4%)
  matrix products  6.73 us (2%)
    ppermute x19, waiting for transfers between devices, swap(): return lax.ppermute(value, 'tensor', partners(members, bit))  121 us
    pallas_call x2, Pallas kernels, forward_slabs(): pl.pallas_call(forward_kernel, grid_spec=pltpu.PrefetchScalarGridSpec(num...  24.9 us
    pallas_call x1, Pallas kernels, add_gradient(): pl.pallas_call(functools.partial(gradient_kernel, steps), grid_spec=pltpu...  23.9 us
    unnamed x50, local copies, waits for them, and re-layouts  17 us
    ppermute x19, starting transfers between devices, swap(): return lax.ppermute(value, 'tensor', partners(members, bit))  14.6 us
    pallas_call x1, Pallas kernels, place_gradients(): pl.pallas_call(functools.partial(place_kernel, ff_slab), grid=(members,),...  9.86 us
    all_to_all x1, starting transfers between devices, local(): lax.all_to_all(packed, 'tensor', 0, 0, tiled=True)  7.56 us
    convert_element_type x3, other arithmetic, send(): return swap(value.astype(wire), members, bit)  7.46 us
  transfers between devices with their start and end apart: 22, of which 9 were waited for; matrix products, arithmetic and copies ran while one was open for 8% of the time, Pallas kernels for 22%

profile of v1, /device:TPU:0, one launch (start us, length us, event | category | flops | bytes accessed | tf_op | source)
XLA Modules:
  0.0 268.8 jit_solution(7875836967777095891)
XLA Ops:
  7.2 0.7 all-gather.3.cloned.1.call-update
  7.9 1.8 copy.22
  9.7 0.5 copy.26
  10.3 0.5 copy-done.15
  10.8 0.2 copy.23
  10.9 0.3 copy.27
  11.2 1.6 pad_maximum_fusion.rest_0_
  12.8 7.6 %all-to-all-start = ((bf16[16,32,2304]{2,1,0:T(8,128)(2,1)}), bf16[16,32,2304]{2,1,0:T(8,128)(2,1)}, u32[]{:S(2)}, u32[]{:S(2)}) async-start(bf16[16,32,2304]{2,1,0:T(8,128)(2,1)} %pad_maximum_fusion.rest_0_), calls=%async_computation | async-start | bytes 4718592 | tf_op jit(solution)/shard_map/all_to_all | solution.py:213
  20.4 12.5 %forward_slabs.3 = f32[8,512,512]{2,1,0:T(8,128)S(1)} custom-call(s32[8]{0:T(128)S(1)} %broadcast_xor_fusion.places, bf16[512,1792]{1,0:T(8,128)(2,1)S(1)} %copy-done.4, bf16[1792,8192]{1,0:T(8,128)(2,1)} %second_ref.1, bf16[16,32,2304]{2,1,0:T(8,128)(2,1)} %pad_maximum_fusion.rest_0_), custom_call_target="tpu_custom_call" | custom-call | flops 7516192768 | bytes 23068672 | tf_op jit(solution)/shard_map/forward_slabs/pallas_call | solution.py:31
  33.0 0.4 slice_bitcast_fusion
  33.4 0.4 collective-permute-start.10
  34.0 0.4 collective-permute-start.7
  34.5 12.4 %forward_slabs.2.rest_0_ = f32[8,512,512]{2,1,0:T(8,128)S(1)} custom-call(s32[8]{0:T(128)S(1)} %broadcast_xor_fusion.1.places, bf16[512,1792]{1,0:T(8,128)(2,1)S(1)} %copy-done.4, bf16[1792,8192]{1,0:T(8,128)(2,1)} %second_ref.1), custom_call_target="tpu_custom_call" | custom-call | flops 7516192768 | bytes 23068672 | tf_op jit(solution)/shard_map/forward_slabs/pallas_call | solution.py:31
  46.9 0.5 slice_bitcast_fusion.8
  47.4 0.4 collective-permute-start
  47.8 0.2 collective-permute-start.1
  48.0 0.4 collective-permute-start.3
  48.3 0.2 collective-permute-start.4
  48.5 4.5 %fusion.3 = (bf16[512,512]{1,0:T(8,128)(2,1)S(1)}, f32[512,512]{1,0:T(8,128)S(1)}, bf16[512,512]{1,0:T(8,128)(2,1)}, f32[512,512]{1,0:T(8,128)S(1)}) fusion(f32[512,512]{1,0:T(8,128)S(1)} %collective-permute-done.11, f32[8,512,512]{2,1,0:T(8,128)S(1)} %forward_slabs.3, f32[512,512]{1,0:T(8,128)S(1)} %collective-permute-done.10, ...), kind=kLoop, calls=%fused_computation.12 | loop fusion | flops 1572864 | bytes 11534336 | tf_op jit(solution)/shard_map/convert_element_type | solution.py:222
  53.0 1.9 collective-permute-start.12
  54.9 18.2 %collective-permute-done.12.other_ref = bf16[512,512]{1,0:T(8,128)(2,1)S(1)} collective-permute-done((bf16[512,512]{1,0:T(8,128)(2,1)S(1)}, bf16[512,512]{1,0:T(8,128)(2,1)S(1)}, u32[]{:S(2)}, u32[]{:S(2)}) %collective-permute-start.12) | collective-permute-done | bytes 524320 | tf_op jit(solution)/shard_map/ppermute | solution.py:20
  73.1 1.1 join.10
  74.1 1.9 collective-permute-start.13
  76.0 1.6 collective-permute-start.9
  77.7 2.1 fusion.9
  79.8 0.3 collective-permute-start.5
  80.1 1.7 collective-permute-start.2
  82.3 23.6 %collective-permute-done.9.other_ref = bf16[512,512]{1,0:T(8,128)(2,1)S(1)} collective-permute-done((bf16[512,512]{1,0:T(8,128)(2,1)}, bf16[512,512]{1,0:T(8,128)(2,1)S(1)}, u32[]{:S(2)}, u32[]{:S(2)}) %collective-permute-start.9) | collective-permute-done | bytes 524320 | tf_op jit(solution)/shard_map/ppermute | solution.py:20
  105.9 3.5 %copy-done.1 = f32[8,512,512]{2,1,0:T(8,128)S(1)} copy-done((f32[8,512,512]{2,1,0:T(8,128)S(1)}, f32[8,512,512]{2,1,0:T(8,128)}, u32[]{:S(2)}) %copy-start.1) | copy-done | bytes 8388632
  109.4 19.0 %collective-permute-done.5.other_ref = bf16[512,512]{1,0:T(8,128)(2,1)} collective-permute-done((bf16[512,512]{1,0:T(8,128)(2,1)}, bf16[512,512]{1,0:T(8,128)(2,1)}, u32[]{:S(2)}, u32[]{:S(2)}) %collective-permute-start.5) | collective-permute-done | bytes 524320 | tf_op jit(solution)/shard_map/ppermute | solution.py:20
  128.5 1.2 join.8.rest_1_
  129.7 1.0 copy-done.9
  130.6 8.9 %collective-permute-done.2.other_ref = bf16[512,512]{1,0:T(8,128)(2,1)} collective-permute-done((bf16[512,512]{1,0:T(8,128)(2,1)}, bf16[512,512]{1,0:T(8,128)(2,1)}, u32[]{:S(2)}, u32[]{:S(2)}) %collective-permute-start.2) | collective-permute-done | bytes 524320 | tf_op jit(solution)/shard_map/ppermute | solution.py:20
  139.5 1.1 join.7.rest_2_.mine_ref
  140.7 1.4 join.11.rest_0_
  142.1 1.0 copy-done.5
  143.1 1.2 copy-done.6
  144.3 1.3 copy-done.10
  145.6 3.1 %low_rank_pair.1 = f32[32,512]{1,0:T(8,128)S(1)} custom-call(bf16[512,2304]{1,0:T(8,128)(2,1)} %bitcast.11.maps_ref, bf16[512,1792]{1,0:T(8,128)(2,1)S(1)} %copy-done.4, bf16[512,512]{1,0:T(8,128)(2,1)S(1)} %copy-done.13, f32[32,1,512]{2,1,0:T(1,128)S(1)} %and_convert_fusion.picker_ref, f32[512,512]{1,0:T(8,128)S(1)} %copy-done.6, ...), custom_call_target="tpu_custom_call" | custom-call | flops 1207959552 | bytes 4718592 | tf_op jit(solution)/shard_map/low_rank_pair/pallas_call | solution.py:174
  148.8 1.2 collective-permute-done.14
  150.1 4.3 %collective-permute-done.15 = f32[32,512]{1,0:T(8,128)S(1)} collective-permute-done((f32[32,512]{1,0:T(8,128)S(1)}, f32[32,512]{1,0:T(8,128)S(1)}, u32[]{:S(2)}, u32[]{:S(2)}) %collective-permute-start.15) | collective-permute-done | bytes 65568 | tf_op jit(solution)/shard_map/ppermute | solution.py:20
  154.4 4.3 %collective-permute-done.16 = f32[32,512]{1,0:T(8,128)S(1)} collective-permute-done((f32[32,512]{1,0:T(8,128)S(1)}, f32[32,512]{1,0:T(8,128)S(1)}, u32[]{:S(2)}, u32[]{:S(2)}) %collective-permute-start.16) | collective-permute-done | bytes 65568 | tf_op jit(solution)/shard_map/ppermute | solution.py:20
  158.7 0.7 collective-permute-start.17
  159.4 4.6 %collective-permute-done.17 = f32[32,512]{1,0:T(8,128)S(1)} collective-permute-done((f32[32,512]{1,0:T(8,128)S(1)}, f32[32,512]{1,0:T(8,128)S(1)}, u32[]{:S(2)}, u32[]{:S(2)}) %collective-permute-start.17) | collective-permute-done | bytes 65568 | tf_op jit(solution)/shard_map/ppermute | solution.py:20
  164.1 0.2 multiply_convert_fusion.2
  164.3 0.4 fusion.1
  164.8 0.4 copy-done.18
  165.3 1.1 multiply_convert_fusion
  166.4 1.6 pad_maximum_fusion.1
  167.9 4.8 %all-to-all-start.1 = ((bf16[16,32,2304]{2,1,0:T(8,128)(2,1)}), bf16[16,32,2304]{2,1,0:T(8,128)(2,1)}, u32[]{:S(2)}, u32[]{:S(2)}) async-start(bf16[16,32,2304]{2,1,0:T(8,128)(2,1)} %bitcast.22.rest_0_), calls=%async_computation.1 | async-start | bytes 4718592 | tf_op jit(solution)/shard_map/all_to_all | solution.py:270
  172.7 1.7 collective-permute-start.6
  174.4 0.9 convert_element_type.75
  175.2 2.4 collective-permute-start.18
  177.7 2.5 convolution_multiply_fusion
  180.2 2.6 multiply_convert_fusion.1.start_ref
  182.9 3.4 %copy-done.8 = bf16[8192,512]{1,0:T(8,128)(2,1)S(1)} copy-done((bf16[8192,512]{1,0:T(8,128)(2,1)S(1)}, bf16[8192,512]{1,0:T(8,128)(2,1)}, u32[]{:S(2)}) %copy-start.8) | copy-done | bytes 8388632
  186.3 23.9 %hidden_gradient.1.rest_0_ = bf16[512,1792]{1,0:T(8,128)(2,1)} custom-call(s32[16]{0:T(128)S(1)} %iota.14.places, bf16[16,512,512]{2,1,0:T(8,128)(2,1)S(1)} %bitcast.79, bf16[1792,8192]{1,0:T(8,128)(2,1)} %second_ref.1, bf16[1792,8192]{1,0:T(8,128)(2,1)} %second_ref.1, bf16[512,1792]{1,0:T(8,128)(2,1)S(1)} %multiply_convert_fusion.1.start_ref, ...), custom_call_target="tpu_custom_call" | custom-call | flops 15032385536 | bytes 37748736 | tf_op jit(solution)/shard_map/hidden_gradient/pallas_call | solution.py:79
  210.2 36.7 %collective-permute-done.6.other_ref = f32[512,512]{1,0:T(8,128)} collective-permute-done((f32[512,512]{1,0:T(8,128)}, f32[512,512]{1,0:T(8,128)}, u32[]{:S(2)}, u32[]{:S(2)}) %collective-permute-start.6) | collective-permute-done | bytes 1048608 | tf_op jit(solution)/shard_map/ppermute | solution.py:20
  246.8 1.5 copy-done.2
  248.3 1.5 join.12.mine_ref
  249.8 0.3 copy-done.3
  250.2 0.9 copy-done.14
  251.1 0.9 add_convert_fusion
  252.0 9.9 %place_gradients.1 = (f32[2,16,28672]{2,1,0:T(8,128)}, f32[2,16,8192]{2,1,0:T(8,128)}) custom-call(bf16[16,32,2304]{2,1,0:T(8,128)(2,1)} %all-to-all-done.1.grads_ref, bf16[512,1792]{1,0:T(8,128)(2,1)S(1)} %copy-done.3), custom_call_target="tpu_custom_call" | custom-call | tf_op jit(solution)/shard_map/place_gradients/pallas_call | solution.py:137
  (72 shorter events, 1.5 us)
Async XLA Ops:
  7.2 175.7 %all-gather.3.cloned.1.call-start = ((), (), s32[]{:S(2)}) async-start(), calls=%async_computation.2 | async-start | bytes 8912896 | tf_op jit(solution)/shard_map/all_gather | solution.py:218
  9.7 1.0 copy-start.15
  12.8 7.6 %copy-start.23 = (s32[8]{0:T(128)S(1)}, s32[8]{0:T(128)}, u32[]{:S(2)}) copy-start(s32[8]{0:T(128)} %constant.3.clone) | copy-start | bytes 100
  12.8 7.6 %copy-start.4 = (bf16[512,1792]{1,0:T(8,128)(2,1)S(1)}, bf16[512,1792]{1,0:T(8,128)(2,1)}, u32[]{:S(2)}) copy-start(bf16[512,1792]{1,0:T(8,128)(2,1)} %hidden_ref.5) | copy-start | bytes 5505028
  12.8 130.3 %all-to-all-start = ((bf16[16,32,2304]{2,1,0:T(8,128)(2,1)}), bf16[16,32,2304]{2,1,0:T(8,128)(2,1)}, u32[]{:S(2)}, u32[]{:S(2)}) async-start(bf16[16,32,2304]{2,1,0:T(8,128)(2,1)} %pad_maximum_fusion.rest_0_), calls=%async_computation | async-start | bytes 4718592 | tf_op jit(solution)/shard_map/all_to_all | solution.py:213
  32.9 1.6 copy-start.22
  33.4 14.4 %collective-permute-start.10 = (f32[512,512]{1,0:T(8,128)S(1)}, f32[512,512]{1,0:T(8,128)S(1)}, u32[]{:S(2)}, u32[]{:S(2)}) collective-permute-start(f32[512,512]{1,0:T(8,128)S(1)} %get-tuple-element.13), channel_id=1, source_target_pairs={{0,1},{1,0},{2,3},{3,2},{4,5},{5,4},{6,7},{7,6},{8,9},{9,8},{10,11... | collective-permute-start | bytes 3145736 | tf_op jit(solution)/shard_map/ppermute | solution.py:20
  33.8 14.1 %collective-permute-start.11 = (f32[512,512]{1,0:T(8,128)S(1)}, f32[512,512]{1,0:T(8,128)S(1)}, u32[]{:S(2)}, u32[]{:S(2)}) collective-permute-start(f32[512,512]{1,0:T(8,128)S(1)} %get-tuple-element.12), channel_id=1, source_target_pairs={{0,1},{1,0},{2,3},{3,2},{4,5},{5,4},{6,7},{7,6},{8,9},{9,8},{10,11... | collective-permute-start | bytes 3145736 | tf_op jit(solution)/shard_map/ppermute | solution.py:20
  34.0 14.3 %collective-permute-start.7 = (f32[512,512]{1,0:T(8,128)S(1)}, f32[512,512]{1,0:T(8,128)}, u32[]{:S(2)}, u32[]{:S(2)}) collective-permute-start(f32[512,512]{1,0:T(8,128)S(1)} %get-tuple-element.15), channel_id=1, source_target_pairs={{0,1},{1,0},{2,3},{3,2},{4,5},{5,4},{6,7},{7,6},{8,9},{9,8},{10,11... | collective-permute-start | bytes 3145736 | tf_op jit(solution)/shard_map/ppermute | solution.py:20
  34.3 14.1 %collective-permute-start.8 = (f32[512,512]{1,0:T(8,128)S(1)}, f32[512,512]{1,0:T(8,128)}, u32[]{:S(2)}, u32[]{:S(2)}) collective-permute-start(f32[512,512]{1,0:T(8,128)S(1)} %get-tuple-element.14), channel_id=1, source_target_pairs={{0,1},{1,0},{2,3},{3,2},{4,5},{5,4},{6,7},{7,6},{8,9},{9,8},{10,11... | collective-permute-start | bytes 3145736 | tf_op jit(solution)/shard_map/ppermute | solution.py:20
  46.9 30.8 %copy-start = (f32[8,512,512]{2,1,0:T(8,128)}, f32[8,512,512]{2,1,0:T(8,128)S(1)}, u32[]{:S(2)}) copy-start(f32[8,512,512]{2,1,0:T(8,128)S(1)} %forward_slabs.2.rest_0_) | copy-start | bytes 25165828
  47.4 28.6 %collective-permute-start = (f32[512,512]{1,0:T(8,128)S(1)}, f32[512,512]{1,0:T(8,128)S(1)}, u32[]{:S(2)}, u32[]{:S(2)}) collective-permute-start(f32[512,512]{1,0:T(8,128)S(1)} %get-tuple-element.23), channel_id=1, source_target_pairs={{0,1},{1,0},{2,3},{3,2},{4,5},{5,4},{6,7},{7,6},{8,9},{9,8},{10,11... | collective-permute-start | bytes 3145736 | tf_op jit(solution)/shard_map/ppermute | solution.py:20
  47.8 29.9 %collective-permute-start.1 = (f32[512,512]{1,0:T(8,128)S(1)}, f32[512,512]{1,0:T(8,128)S(1)}, u32[]{:S(2)}, u32[]{:S(2)}) collective-permute-start(f32[512,512]{1,0:T(8,128)S(1)} %get-tuple-element.22), channel_id=1, source_target_pairs={{0,1},{1,0},{2,3},{3,2},{4,5},{5,4},{6,7},{7,6},{8,9},{9,8},{10,11... | collective-permute-start | bytes 3145736 | tf_op jit(solution)/shard_map/ppermute | solution.py:20
  48.0 29.7 %collective-permute-start.3 = (f32[512,512]{1,0:T(8,128)S(1)}, f32[512,512]{1,0:T(8,128)S(1)}, u32[]{:S(2)}, u32[]{:S(2)}) collective-permute-start(f32[512,512]{1,0:T(8,128)S(1)} %get-tuple-element.21), channel_id=1, source_target_pairs={{0,1},{1,0},{2,3},{3,2},{4,5},{5,4},{6,7},{7,6},{8,9},{9,8},{10,11... | collective-permute-start | bytes 3145736 | tf_op jit(solution)/shard_map/ppermute | solution.py:20
  48.3 29.4 %collective-permute-start.4 = (f32[512,512]{1,0:T(8,128)S(1)}, f32[512,512]{1,0:T(8,128)S(1)}, u32[]{:S(2)}, u32[]{:S(2)}) collective-permute-start(f32[512,512]{1,0:T(8,128)S(1)} %get-tuple-element.20), channel_id=1, source_target_pairs={{0,1},{1,0},{2,3},{3,2},{4,5},{5,4},{6,7},{7,6},{8,9},{9,8},{10,11... | collective-permute-start | bytes 3145736 | tf_op jit(solution)/shard_map/ppermute | solution.py:20
  53.0 20.1 %collective-permute-start.12 = (bf16[512,512]{1,0:T(8,128)(2,1)S(1)}, bf16[512,512]{1,0:T(8,128)(2,1)S(1)}, u32[]{:S(2)}, u32[]{:S(2)}) collective-permute-start(bf16[512,512]{1,0:T(8,128)(2,1)S(1)} %get-tuple-element.8), channel_id=1, source_target_pairs={{0,2},{1,3},{2,0},{3,1},{4,6},{5,7},{6,4},{7,5},{8,10},{9,11},{10,... | collective-permute-start | bytes 1572872 | tf_op jit(solution)/shard_map/ppermute | solution.py:20
  74.1 66.5 %collective-permute-start.13 = (f32[512,512]{1,0:T(8,128)}, f32[512,512]{1,0:T(8,128)}, u32[]{:S(2)}, u32[]{:S(2)}) collective-permute-start(f32[512,512]{1,0:T(8,128)} %join.10), channel_id=1, source_target_pairs={{0,4},{1,5},{2,6},{3,7},{4,0},{5,1},{6,2},{7,3},{8,12},{9,13},{10,... | collective-permute-start | bytes 3145736 | tf_op jit(solution)/shard_map/ppermute | solution.py:20
  76.0 5.8 %copy-start.20 = (s32[64]{0:T(128)S(1)}, s32[64]{0:T(128)}, u32[]{:S(2)}) copy-start(s32[64]{0:T(128)} %param.13) | copy-start | bytes 772
  76.0 6.0 %copy-start.21 = (s32[64]{0:T(128)S(1)}, s32[64]{0:T(128)}, u32[]{:S(2)}) copy-start(s32[64]{0:T(128)} %param.14) | copy-start | bytes 772
  76.0 29.8 %collective-permute-start.9 = (bf16[512,512]{1,0:T(8,128)(2,1)}, bf16[512,512]{1,0:T(8,128)(2,1)S(1)}, u32[]{:S(2)}, u32[]{:S(2)}) collective-permute-start(bf16[512,512]{1,0:T(8,128)(2,1)} %get-tuple-element.10), channel_id=1, source_target_pairs={{0,2},{1,3},{2,0},{3,1},{4,6},{5,7},{6,4},{7,5},{8,10},{9,11},{10,... | collective-permute-start | bytes 1572872 | tf_op jit(solution)/shard_map/ppermute | solution.py:20
  79.8 48.7 %collective-permute-start.5 = (bf16[512,512]{1,0:T(8,128)(2,1)}, bf16[512,512]{1,0:T(8,128)(2,1)}, u32[]{:S(2)}, u32[]{:S(2)}) collective-permute-start(bf16[512,512]{1,0:T(8,128)(2,1)} %get-tuple-element.16), channel_id=1, source_target_pairs={{0,2},{1,3},{2,0},{3,1},{4,6},{5,7},{6,4},{7,5},{8,10},{9,11},{10,... | collective-permute-start | bytes 1572872 | tf_op jit(solution)/shard_map/ppermute | solution.py:20
  80.1 59.4 %collective-permute-start.2 = (bf16[512,512]{1,0:T(8,128)(2,1)}, bf16[512,512]{1,0:T(8,128)(2,1)}, u32[]{:S(2)}, u32[]{:S(2)}) collective-permute-start(bf16[512,512]{1,0:T(8,128)(2,1)} %get-tuple-element.18), channel_id=1, source_target_pairs={{0,2},{1,3},{2,0},{3,1},{4,6},{5,7},{6,4},{7,5},{8,10},{9,11},{10,... | collective-permute-start | bytes 1572872 | tf_op jit(solution)/shard_map/ppermute | solution.py:20
  105.9 3.5 %copy-start.1 = (f32[8,512,512]{2,1,0:T(8,128)S(1)}, f32[8,512,512]{2,1,0:T(8,128)}, u32[]{:S(2)}) copy-start(f32[8,512,512]{2,1,0:T(8,128)} %copy-done) | copy-start | bytes 25165828
  109.3 19.1 %copy-start.12 = (f32[512,512]{1,0:T(8,128)S(1)}, f32[512,512]{1,0:T(8,128)}, u32[]{:S(2)}) copy-start(f32[512,512]{1,0:T(8,128)} %get-tuple-element.17.mine_ref) | copy-start | bytes 3145732
  128.5 11.1 %copy-start.11 = (f32[512,512]{1,0:T(8,128)S(1)}, f32[512,512]{1,0:T(8,128)}, u32[]{:S(2)}) copy-start(f32[512,512]{1,0:T(8,128)} %get-tuple-element.19.mine_ref) | copy-start | bytes 3145732
  129.7 1.0 copy-start.9
  140.7 2.4 copy-start.13
  142.1 1.0 copy-start.5
  143.1 1.2 copy-start.6
  144.3 1.3 copy-start.10
  148.7 1.3 collective-permute-start.14
  150.0 4.3 %collective-permute-start.15 = (f32[32,512]{1,0:T(8,128)S(1)}, f32[32,512]{1,0:T(8,128)S(1)}, u32[]{:S(2)}, u32[]{:S(2)}) collective-permute-start(f32[32,512]{1,0:T(8,128)S(1)} %add.47), channel_id=1, source_target_pairs={{0,2},{1,3},{2,0},{3,1},{4,6},{5,7},{6,4},{7,5},{8,10},{9,11},{10,... | collective-permute-start | bytes 196616 | tf_op jit(solution)/shard_map/ppermute | solution.py:20
  154.4 4.3 %collective-permute-start.16 = (f32[32,512]{1,0:T(8,128)S(1)}, f32[32,512]{1,0:T(8,128)S(1)}, u32[]{:S(2)}, u32[]{:S(2)}) collective-permute-start(f32[32,512]{1,0:T(8,128)S(1)} %add.48), channel_id=1, source_target_pairs={{0,4},{1,5},{2,6},{3,7},{4,0},{5,1},{6,2},{7,3},{8,12},{9,13},{10,... | collective-permute-start | bytes 196616 | tf_op jit(solution)/shard_map/ppermute | solution.py:20
  158.7 5.4 %collective-permute-start.17 = (f32[32,512]{1,0:T(8,128)S(1)}, f32[32,512]{1,0:T(8,128)S(1)}, u32[]{:S(2)}, u32[]{:S(2)}) collective-permute-start(f32[32,512]{1,0:T(8,128)S(1)} %add.49), channel_id=1, source_target_pairs={{0,8},{1,9},{2,10},{3,11},{4,12},{5,13},{6,14},{7,15},{8,0},{9,1},... | collective-permute-start | bytes 196616 | tf_op jit(solution)/shard_map/ppermute | solution.py:20
  164.3 0.8 copy-start.18
  164.3 1.0 copy-start.16
  167.9 6.4 %copy-start.7 = (f32[512,512]{1,0:T(8,128)S(1)}, f32[512,512]{1,0:T(8,128)}, u32[]{:S(2)}) copy-start(f32[512,512]{1,0:T(8,128)} %copy-done.5) | copy-start | bytes 3145732
  167.9 9.7 %copy-start.19 = (bf16[32,16,512]{2,1,0:T(8,128)(2,1)S(1)}, bf16[32,16,512]{2,1,0:T(8,128)(2,1)}, u32[]{:S(2)}) copy-start(bf16[32,16,512]{2,1,0:T(8,128)(2,1)} %copy-done.18) | copy-start | bytes 1572868
  167.9 84.1 %all-to-all-start.1 = ((bf16[16,32,2304]{2,1,0:T(8,128)(2,1)}), bf16[16,32,2304]{2,1,0:T(8,128)(2,1)}, u32[]{:S(2)}, u32[]{:S(2)}) async-start(bf16[16,32,2304]{2,1,0:T(8,128)(2,1)} %bitcast.22.rest_0_), calls=%async_computation.1 | async-start | bytes 4718592 | tf_op jit(solution)/shard_map/all_to_all | solution.py:270
  172.7 7.5 %copy-start.17 = (bf16[32,16,512]{2,1,0:T(8,128)(2,1)S(1)}, bf16[32,16,512]{2,1,0:T(8,128)(2,1)}, u32[]{:S(2)}) copy-start(bf16[32,16,512]{2,1,0:T(8,128)(2,1)} %copy-done.16) | copy-start | bytes 1572868
  172.7 74.1 %collective-permute-start.6 = (f32[512,512]{1,0:T(8,128)}, f32[512,512]{1,0:T(8,128)}, u32[]{:S(2)}, u32[]{:S(2)}) collective-permute-start(f32[512,512]{1,0:T(8,128)} %copy-done.9), channel_id=1, source_target_pairs={{0,4},{1,5},{2,6},{3,7},{4,0},{5,1},{6,2},{7,3},{8,12},{9,13},{10,... | collective-permute-start | bytes 3145736 | tf_op jit(solution)/shard_map/ppermute | solution.py:20
  175.2 74.6 %collective-permute-start.18 = (bf16[512,512]{1,0:T(8,128)(2,1)}, bf16[512,512]{1,0:T(8,128)(2,1)S(1)}, u32[]{:S(2)}, u32[]{:S(2)}) collective-permute-start(bf16[512,512]{1,0:T(8,128)(2,1)} %convert_element_type.75), channel_id=1, source_target_pairs={{0,8},{1,9},{2,10},{3,11},{4,12},{5,13},{6,14},{7,15},{8,0},{9,1},... | collective-permute-start | bytes 1572872 | tf_op jit(solution)/shard_map/ppermute | solution.py:20
  182.9 3.4 %copy-start.8 = (bf16[8192,512]{1,0:T(8,128)(2,1)S(1)}, bf16[8192,512]{1,0:T(8,128)(2,1)}, u32[]{:S(2)}) copy-start(bf16[8192,512]{1,0:T(8,128)(2,1)} %all-gather.3.cloned.1.call-done) | copy-start | bytes 25165828
  246.8 1.5 copy-start.2
  248.3 1.8 copy-start.3
  249.8 1.3 copy-start.14
Sparse Core Ops, SparseCore 0:
  10.2 135.5 all-gather.2

commit v2 on v1

--- a/solution.py
+++ b/solution.py
@@ -115,19 +115,33 @@
 
 
 def join_kernel(mine_ref, other_ref, *rest):
-    rest[-1][...] = mine_ref[...] + other_ref[...].astype(jnp.float32)
-
-
-def join(mine, other, earlier):
-    shape = jax.ShapeDtypeStruct(mine.shape, jnp.float32)
+    total = mine_ref[...] + other_ref[...].astype(jnp.float32)
+    rest[-1][...] = total.astype(rest[-1].dtype)
+
+
+def join(mine, other, earlier, dtype=jnp.float32):
+    shape = jax.ShapeDtypeStruct(mine.shape, dtype)
     return whole_call(join_kernel, (mine, other), shape, earlier, "join")
+
+
+def gate_kernel(value_ref, *rest):
+    rest[-1][...] = value_ref[...]
+
+
+def gate(value, earlier):
+    shape = jax.ShapeDtypeStruct(value.shape, value.dtype)
+    return whole_call(gate_kernel, (value,), shape, earlier, "gate")
 
 
 def place_kernel(ff_slab, grads_ref, *rest):
     in_ref, out_ref = rest[-2:]
-    grads = grads_ref[0].astype(jnp.float32)
-    in_ref[...] = grads[:, :ff_slab].reshape(in_ref.shape)
-    out_ref[...] = grads[:, ff_slab:].reshape(out_ref.shape)
+    resident, rank_width, _ = in_ref.shape
+    count, _, width = grads_ref.shape
+    d_slab = width - ff_slab
+    for m in range(count):
+        grads = grads_ref[m].astype(jnp.float32).reshape(resident, rank_width, width)
+        in_ref[:, :, m * ff_slab : (m + 1) * ff_slab] = grads[:, :, :ff_slab]
+        out_ref[:, :, m * d_slab : (m + 1) * d_slab] = grads[:, :, ff_slab:]
 
 
 def place_gradients(grads, resident, ff_slab, earlier):
@@ -136,12 +150,12 @@
     d_slab = width - ff_slab
     return pl.pallas_call(
         functools.partial(place_kernel, ff_slab),
-        grid=(members,),
-        in_specs=[pl.BlockSpec((1, held_rows, width), lambda m: (m, 0, 0))]
+        grid=(members // 4,),
+        in_specs=[pl.BlockSpec((4, held_rows, width), lambda m: (m, 0, 0))]
         + [pl.BlockSpec(memory_space=pl.ANY)] * len(earlier),
         out_specs=[
-            pl.BlockSpec((resident, rank_width, ff_slab), lambda m: (0, 0, m)),
-            pl.BlockSpec((resident, rank_width, d_slab), lambda m: (0, 0, m)),
+            pl.BlockSpec((resident, rank_width, 4 * ff_slab), lambda m: (0, 0, m)),
+            pl.BlockSpec((resident, rank_width, 4 * d_slab), lambda m: (0, 0, m)),
         ],
         out_shape=[
             jax.ShapeDtypeStruct((resident, rank_width, members * ff_slab), jnp.float32),
@@ -243,7 +257,10 @@
     for bit in bits[1:-1]:
         for k in [k for k in sums if k % (2 * bit) == bit]:
             if k >= half or bit == bits[1]:
-                sums[k ^ bit] = join(sums[k ^ bit], send(sums[k], bit), groups[1:])
+                last = k ^ bit == half and bit == bits[-2]
+                dtype = jnp.bfloat16 if last and half in narrow_bits else jnp.float32
+                sums[k ^ bit] = join(sums[k ^ bit], send(sums[k], bit), groups[1:], dtype)
+    last_sent = send(sums[half], half)
     ready = (sums[half],) + tuple(
         sums[k] for k in sums if k < half and k % (2 * bits[1]) == 0
     )
@@ -256,6 +273,7 @@
     pair = low_rank_pair(maps, hidden, cotangent, picker, ready)
     for bit in bits:
         pair = pair + swap(pair, members, bit)
+    pair = gate(pair, (last_sent,))
     pair = pair.astype(jnp.bfloat16).astype(jnp.float32)
     flat = (adapters * rank_width, tokens)
     low_spread = (picker * pair[None, :rank_width]).astype(jnp.bfloat16).reshape(flat)
@@ -281,7 +299,7 @@
     for bit in bits[2:-1]:
         for k in [k for k in sums if k < half and k % (2 * bit) == bit]:
             sums[k ^ bit] = join(sums[k ^ bit], send(sums[k], bit), (hidden_gradient,))
-    output_sum = join(sums[0], send(sums[half], half), (hidden_gradient,))
+    output_sum = join(sums[0], last_sent, (hidden_gradient,))
     input_map_gradient, output_map_gradient = place_gradients(
         grads, resident, ff_slab, (hidden_gradient,)
     )

time: 270 us -> 261 us (0.967)
  Pallas kernels: 68.2 us -> 64.6 us
    pallas_call x1, Pallas kernels: 9.86 us -> 4.34 us  [place_gradients(): pl.pallas_call(functools.partial(place_kernel, ff_slab), grid=(members //...]
    unnamed x50 -> x48, local copies, waits for them, and re-layouts: 17 us -> 14.6 us
    pallas_call x7 -> x8, Pallas kernels: 6.44 us -> 8.36 us  [whole_call(): pl.pallas_call(kernel, in_specs=[pl.BlockSpec(memory_space=pltpu.VMEM)] *...]
    convert_element_type x3 -> x2, other arithmetic: 7.46 us -> 5.65 us  [send(): return swap(value.astype(wire), members, bit)]
  transfers between devices with their start and end apart: 22 -> 22, of which waited for: 9 -> 9; matrix products, arithmetic and copies ran while one was open for 8% -> 8% of each run, Pallas kernels for 22% -> 23%
where the time goes in v2:
time: 261 us; the launch traced here: 260 us
  waiting for transfers between devices  121 us (46%)
  Pallas kernels  64.6 us (25%)
  starting transfers between devices  25.4 us (10%)
  local copies, waits for them, and re-layouts  16.6 us (6%)
  between operations  14.4 us (6%)
  other arithmetic  10.1 us (4%)
  matrix products  7.9 us (3%)
    ppermute x19, waiting for transfers between devices, swap(): return lax.ppermute(value, 'tensor', partners(members, bit))  120 us
    pallas_call x2, Pallas kernels, forward_slabs(): pl.pallas_call(forward_kernel, grid_spec=pltpu.PrefetchScalarGridSpec(num...  24.9 us
    pallas_call x1, Pallas kernels, add_gradient(): pl.pallas_call(functools.partial(gradient_kernel, steps), grid_spec=pltpu...  23.9 us
    unnamed x48, local copies, waits for them, and re-layouts  14.6 us
    ppermute x19, starting transfers between devices, swap(): return lax.ppermute(value, 'tensor', partners(members, bit))  13.1 us
    pallas_call x8, Pallas kernels, whole_call(): pl.pallas_call(kernel, in_specs=[pl.BlockSpec(memory_space=pltpu.VMEM)] *...  8.36 us
    all_to_all x1, starting transfers between devices, local(): lax.all_to_all(packed, 'tensor', 0, 0, tiled=True)  7.56 us
    convert_element_type x2, other arithmetic, send(): return swap(value.astype(wire), members, bit)  5.65 us
  transfers between devices with their start and end apart: 22, of which 9 were waited for; matrix products, arithmetic and copies ran while one was open for 8% of the time, Pallas kernels for 23%

profile of v2, /device:TPU:0, one launch (start us, length us, event | category | flops | bytes accessed | tf_op | source)
XLA Modules:
  0.0 259.6 jit_solution(5547245375537327211)
XLA Ops:
  7.2 0.7 all-gather.3.cloned.1.call-update
  7.9 1.8 copy.22
  9.7 0.5 copy.26
  10.3 0.5 copy-done.14
  10.8 0.2 copy.23
  10.9 0.3 copy.27
  11.2 1.6 pad_maximum_fusion.rest_0_
  12.8 7.6 %all-to-all-start = ((bf16[16,32,2304]{2,1,0:T(8,128)(2,1)}), bf16[16,32,2304]{2,1,0:T(8,128)(2,1)}, u32[]{:S(2)}, u32[]{:S(2)}) async-start(bf16[16,32,2304]{2,1,0:T(8,128)(2,1)} %pad_maximum_fusion.rest_0_), calls=%async_computation | async-start | bytes 4718592 | tf_op jit(solution)/shard_map/all_to_all | solution.py:227
  20.4 12.5 %forward_slabs.3 = f32[8,512,512]{2,1,0:T(8,128)S(1)} custom-call(s32[8]{0:T(128)S(1)} %broadcast_xor_fusion.places, bf16[512,1792]{1,0:T(8,128)(2,1)S(1)} %copy-done.4, bf16[1792,8192]{1,0:T(8,128)(2,1)} %second_ref.1, bf16[16,32,2304]{2,1,0:T(8,128)(2,1)} %pad_maximum_fusion.rest_0_), custom_call_target="tpu_custom_call" | custom-call | flops 7516192768 | bytes 23068672 | tf_op jit(solution)/shard_map/forward_slabs/pallas_call | solution.py:31
  33.0 0.4 slice_bitcast_fusion
  33.4 0.4 collective-permute-start.10
  34.0 0.4 collective-permute-start.7
  34.5 12.4 %forward_slabs.2.rest_0_ = f32[8,512,512]{2,1,0:T(8,128)S(1)} custom-call(s32[8]{0:T(128)S(1)} %broadcast_xor_fusion.1.places, bf16[512,1792]{1,0:T(8,128)(2,1)S(1)} %copy-done.4, bf16[1792,8192]{1,0:T(8,128)(2,1)} %second_ref.1), custom_call_target="tpu_custom_call" | custom-call | flops 7516192768 | bytes 23068672 | tf_op jit(solution)/shard_map/forward_slabs/pallas_call | solution.py:31
  46.9 0.5 slice_bitcast_fusion.8
  47.4 0.4 collective-permute-start
  47.8 0.2 collective-permute-start.1
  48.0 0.4 collective-permute-start.3
  48.3 0.2 collective-permute-start.4
  48.5 3.6 %fusion.3 = (bf16[512,512]{1,0:T(8,128)(2,1)S(1)}, f32[512,512]{1,0:T(8,128)S(1)}, bf16[512,512]{1,0:T(8,128)(2,1)}, f32[512,512]{1,0:T(8,128)S(1)}) fusion(f32[512,512]{1,0:T(8,128)S(1)} %collective-permute-done.11, f32[8,512,512]{2,1,0:T(8,128)S(1)} %forward_slabs.3, f32[512,512]{1,0:T(8,128)S(1)} %collective-permute-done.10, ...), kind=kLoop, calls=%fused_computation.12 | loop fusion | flops 1572864 | bytes 11534336 | tf_op jit(solution)/shard_map/convert_element_type | solution.py:236
  52.1 1.9 collective-permute-start.12
  54.0 18.6 %collective-permute-done.12.other_ref = bf16[512,512]{1,0:T(8,128)(2,1)S(1)} collective-permute-done((bf16[512,512]{1,0:T(8,128)(2,1)S(1)}, bf16[512,512]{1,0:T(8,128)(2,1)S(1)}, u32[]{:S(2)}, u32[]{:S(2)}) %collective-permute-start.12) | collective-permute-done | bytes 524320 | tf_op jit(solution)/shard_map/ppermute | solution.py:20
  72.6 1.1 join.10
  73.6 2.1 collective-permute-start.13
  75.8 0.4 collective-permute-start.9
  76.2 2.0 fusion.9
  78.3 1.6 collective-permute-start.5
  79.8 0.4 collective-permute-start.2
  80.7 25.1 %collective-permute-done.9.other_ref = bf16[512,512]{1,0:T(8,128)(2,1)S(1)} collective-permute-done((bf16[512,512]{1,0:T(8,128)(2,1)}, bf16[512,512]{1,0:T(8,128)(2,1)S(1)}, u32[]{:S(2)}, u32[]{:S(2)}) %collective-permute-start.9) | collective-permute-done | bytes 524320 | tf_op jit(solution)/shard_map/ppermute | solution.py:20
  105.9 3.5 %copy-done.1 = f32[8,512,512]{2,1,0:T(8,128)S(1)} copy-done((f32[8,512,512]{2,1,0:T(8,128)S(1)}, f32[8,512,512]{2,1,0:T(8,128)}, u32[]{:S(2)}) %copy-start.1) | copy-done | bytes 8388632
  109.4 19.0 %collective-permute-done.5.other_ref = bf16[512,512]{1,0:T(8,128)(2,1)} collective-permute-done((bf16[512,512]{1,0:T(8,128)(2,1)}, bf16[512,512]{1,0:T(8,128)(2,1)}, u32[]{:S(2)}, u32[]{:S(2)}) %collective-permute-start.5) | collective-permute-done | bytes 524320 | tf_op jit(solution)/shard_map/ppermute | solution.py:20
  128.4 1.2 join.8.rest_1_
  129.7 9.9 %collective-permute-done.2.other_ref = bf16[512,512]{1,0:T(8,128)(2,1)} collective-permute-done((bf16[512,512]{1,0:T(8,128)(2,1)}, bf16[512,512]{1,0:T(8,128)(2,1)}, u32[]{:S(2)}, u32[]{:S(2)}) %collective-permute-start.2) | collective-permute-done | bytes 524320 | tf_op jit(solution)/shard_map/ppermute | solution.py:20
  139.6 1.1 join.7.rest_2_.mine_ref
  140.7 2.2 join.11.rest_0_
  142.9 0.5 collective-permute-start.18
  143.4 1.2 copy-done.7
  144.6 3.1 %low_rank_pair.1 = f32[32,512]{1,0:T(8,128)S(1)} custom-call(bf16[512,2304]{1,0:T(8,128)(2,1)} %bitcast.11.maps_ref, bf16[512,1792]{1,0:T(8,128)(2,1)S(1)} %copy-done.4, bf16[512,512]{1,0:T(8,128)(2,1)S(1)} %copy-done.11, f32[32,1,512]{2,1,0:T(1,128)S(1)} %and_convert_fusion.picker_ref, bf16[512,512]{1,0:T(8,128)(2,1)} %join.11.rest_0_, ...), custom_call_target="tpu_custom_call" | custom-call | flops 1207959552 | bytes 4718592 | tf_op jit(solution)/shard_map/low_rank_pair/pallas_call | solution.py:188
  147.8 1.2 collective-permute-done.14
  149.0 1.7 collective-permute-start.15
  150.7 2.6 %collective-permute-done.15 = f32[32,512]{1,0:T(8,128)S(1)} collective-permute-done((f32[32,512]{1,0:T(8,128)S(1)}, f32[32,512]{1,0:T(8,128)S(1)}, u32[]{:S(2)}, u32[]{:S(2)}) %collective-permute-start.15) | collective-permute-done | bytes 65568 | tf_op jit(solution)/shard_map/ppermute | solution.py:20
  153.4 0.4 collective-permute-start.16
  153.8 7.5 %collective-permute-done.16 = f32[32,512]{1,0:T(8,128)S(1)} collective-permute-done((f32[32,512]{1,0:T(8,128)S(1)}, f32[32,512]{1,0:T(8,128)S(1)}, u32[]{:S(2)}, u32[]{:S(2)}) %collective-permute-start.16) | collective-permute-done | bytes 65568 | tf_op jit(solution)/shard_map/ppermute | solution.py:20
  161.4 9.4 %collective-permute-done.17 = f32[32,512]{1,0:T(8,128)S(1)} collective-permute-done((f32[32,512]{1,0:T(8,128)S(1)}, f32[32,512]{1,0:T(8,128)S(1)}, u32[]{:S(2)}, u32[]{:S(2)}) %collective-permute-start.17) | collective-permute-done | bytes 65568 | tf_op jit(solution)/shard_map/ppermute | solution.py:20
  170.8 0.2 multiply_convert_fusion.2
  171.1 0.4 fusion.1
  171.5 0.3 copy-done.17
  171.8 0.2 copy-done.15
  172.0 1.1 multiply_convert_fusion
  173.1 1.6 pad_maximum_fusion.1
  174.7 4.8 %all-to-all-start.1 = ((bf16[16,32,2304]{2,1,0:T(8,128)(2,1)}), bf16[16,32,2304]{2,1,0:T(8,128)(2,1)}, u32[]{:S(2)}, u32[]{:S(2)}) async-start(bf16[16,32,2304]{2,1,0:T(8,128)(2,1)} %bitcast.22.rest_0_), calls=%async_computation.1 | async-start | bytes 4718592 | tf_op jit(solution)/shard_map/all_to_all | solution.py:288
  179.5 1.7 collective-permute-start.6
  181.1 2.5 convolution_multiply_fusion
  183.6 3.9 %multiply_convert_fusion.1.start_ref = bf16[512,1792]{1,0:T(8,128)(2,1)} fusion(bf16[512,512]{1,0:T(8,128)(2,1)S(1)} %bitcast.87, bf16[512,2304]{1,0:T(8,128)(2,1)} %bitcast.11.maps_ref), kind=kOutput, calls=%fused_computation.1 | convolution fusion | flops 941359104 | bytes 4194304 | tf_op jit(solution)/shard_map/dot_general | solution.py:293
  187.5 3.4 %copy-done.5 = bf16[8192,512]{1,0:T(8,128)(2,1)S(1)} copy-done((bf16[8192,512]{1,0:T(8,128)(2,1)S(1)}, bf16[8192,512]{1,0:T(8,128)(2,1)}, u32[]{:S(2)}) %copy-start.5) | copy-done | bytes 8388632
  190.9 1.5 copy-done.12
  192.4 23.9 %hidden_gradient.1.rest_0_ = bf16[512,1792]{1,0:T(8,128)(2,1)} custom-call(s32[16]{0:T(128)S(1)} %iota.14.places, bf16[16,512,512]{2,1,0:T(8,128)(2,1)S(1)} %bitcast.79, bf16[1792,8192]{1,0:T(8,128)(2,1)} %second_ref.1, bf16[1792,8192]{1,0:T(8,128)(2,1)} %second_ref.1, bf16[512,1792]{1,0:T(8,128)(2,1)S(1)} %copy-done.12, bf16[16,32,2304]{2,1,0:T(8,128)(2,1)} %bitcast.22.rest_0_), custom_call_target="tpu_custom_call" | custom-call | flops 15032385536 | bytes 37748736 | tf_op jit(solution)/shard_map/hidden_gradient/pallas_call | solution.py:79
  216.2 26.5 %collective-permute-done.6.other_ref = f32[512,512]{1,0:T(8,128)} collective-permute-done((f32[512,512]{1,0:T(8,128)S(1)}, f32[512,512]{1,0:T(8,128)}, u32[]{:S(2)}, u32[]{:S(2)}) %collective-permute-start.6) | collective-permute-done | bytes 1048608 | tf_op jit(solution)/shard_map/ppermute | solution.py:20
  242.8 1.5 copy-done.2
  244.3 1.5 join.12.mine_ref
  245.7 0.3 copy-done.3
  246.1 1.2 join.13
  247.3 0.2 copy-done.13
  247.5 0.9 add_convert_fusion
  248.4 4.3 %place_gradients.1 = (f32[2,16,28672]{2,1,0:T(8,128)}, f32[2,16,8192]{2,1,0:T(8,128)}) custom-call(bf16[16,32,2304]{2,1,0:T(8,128)(2,1)} %all-to-all-done.1.grads_ref, bf16[512,1792]{1,0:T(8,128)(2,1)S(1)} %copy-done.3), custom_call_target="tpu_custom_call" | custom-call | tf_op jit(solution)/shard_map/place_gradients/pallas_call | solution.py:151
  (71 shorter events, 1.2 us)
Async XLA Ops:
  7.2 180.3 %all-gather.3.cloned.1.call-start = ((), (), s32[]{:S(2)}) async-start(), calls=%async_computation.2 | async-start | bytes 8912896 | tf_op jit(solution)/shard_map/all_gather | solution.py:232
  9.7 1.0 copy-start.14
  12.8 7.6 %copy-start.22 = (s32[8]{0:T(128)S(1)}, s32[8]{0:T(128)}, u32[]{:S(2)}) copy-start(s32[8]{0:T(128)} %constant.3.clone) | copy-start | bytes 100
  12.8 7.6 %copy-start.4 = (bf16[512,1792]{1,0:T(8,128)(2,1)S(1)}, bf16[512,1792]{1,0:T(8,128)(2,1)}, u32[]{:S(2)}) copy-start(bf16[512,1792]{1,0:T(8,128)(2,1)} %hidden_ref.5) | copy-start | bytes 5505028
  12.8 130.6 %all-to-all-start = ((bf16[16,32,2304]{2,1,0:T(8,128)(2,1)}), bf16[16,32,2304]{2,1,0:T(8,128)(2,1)}, u32[]{:S(2)}, u32[]{:S(2)}) async-start(bf16[16,32,2304]{2,1,0:T(8,128)(2,1)} %pad_maximum_fusion.rest_0_), calls=%async_computation | async-start | bytes 4718592 | tf_op jit(solution)/shard_map/all_to_all | solution.py:227
  32.9 1.6 copy-start.21
  33.4 14.4 %collective-permute-start.10 = (f32[512,512]{1,0:T(8,128)S(1)}, f32[512,512]{1,0:T(8,128)S(1)}, u32[]{:S(2)}, u32[]{:S(2)}) collective-permute-start(f32[512,512]{1,0:T(8,128)S(1)} %get-tuple-element.13), channel_id=1, source_target_pairs={{0,1},{1,0},{2,3},{3,2},{4,5},{5,4},{6,7},{7,6},{8,9},{9,8},{10,11... | collective-permute-start | bytes 3145736 | tf_op jit(solution)/shard_map/ppermute | solution.py:20
  33.8 14.1 %collective-permute-start.11 = (f32[512,512]{1,0:T(8,128)S(1)}, f32[512,512]{1,0:T(8,128)S(1)}, u32[]{:S(2)}, u32[]{:S(2)}) collective-permute-start(f32[512,512]{1,0:T(8,128)S(1)} %get-tuple-element.12), channel_id=1, source_target_pairs={{0,1},{1,0},{2,3},{3,2},{4,5},{5,4},{6,7},{7,6},{8,9},{9,8},{10,11... | collective-permute-start | bytes 3145736 | tf_op jit(solution)/shard_map/ppermute | solution.py:20
  34.0 14.3 %collective-permute-start.7 = (f32[512,512]{1,0:T(8,128)S(1)}, f32[512,512]{1,0:T(8,128)S(1)}, u32[]{:S(2)}, u32[]{:S(2)}) collective-permute-start(f32[512,512]{1,0:T(8,128)S(1)} %get-tuple-element.15), channel_id=1, source_target_pairs={{0,1},{1,0},{2,3},{3,2},{4,5},{5,4},{6,7},{7,6},{8,9},{9,8},{10,11... | collective-permute-start | bytes 3145736 | tf_op jit(solution)/shard_map/ppermute | solution.py:20
  34.3 14.1 %collective-permute-start.8 = (f32[512,512]{1,0:T(8,128)S(1)}, f32[512,512]{1,0:T(8,128)}, u32[]{:S(2)}, u32[]{:S(2)}) collective-permute-start(f32[512,512]{1,0:T(8,128)S(1)} %get-tuple-element.14), channel_id=1, source_target_pairs={{0,1},{1,0},{2,3},{3,2},{4,5},{5,4},{6,7},{7,6},{8,9},{9,8},{10,11... | collective-permute-start | bytes 3145736 | tf_op jit(solution)/shard_map/ppermute | solution.py:20
  46.9 29.3 %copy-start = (f32[8,512,512]{2,1,0:T(8,128)}, f32[8,512,512]{2,1,0:T(8,128)S(1)}, u32[]{:S(2)}) copy-start(f32[8,512,512]{2,1,0:T(8,128)S(1)} %forward_slabs.2.rest_0_) | copy-start | bytes 25165828
  47.4 28.4 %collective-permute-start = (f32[512,512]{1,0:T(8,128)S(1)}, f32[512,512]{1,0:T(8,128)S(1)}, u32[]{:S(2)}, u32[]{:S(2)}) collective-permute-start(f32[512,512]{1,0:T(8,128)S(1)} %get-tuple-element.23), channel_id=1, source_target_pairs={{0,1},{1,0},{2,3},{3,2},{4,5},{5,4},{6,7},{7,6},{8,9},{9,8},{10,11... | collective-permute-start | bytes 3145736 | tf_op jit(solution)/shard_map/ppermute | solution.py:20
  47.8 28.4 %collective-permute-start.1 = (f32[512,512]{1,0:T(8,128)S(1)}, f32[512,512]{1,0:T(8,128)S(1)}, u32[]{:S(2)}, u32[]{:S(2)}) collective-permute-start(f32[512,512]{1,0:T(8,128)S(1)} %get-tuple-element.22), channel_id=1, source_target_pairs={{0,1},{1,0},{2,3},{3,2},{4,5},{5,4},{6,7},{7,6},{8,9},{9,8},{10,11... | collective-permute-start | bytes 3145736 | tf_op jit(solution)/shard_map/ppermute | solution.py:20
  48.0 28.2 %collective-permute-start.3 = (f32[512,512]{1,0:T(8,128)S(1)}, f32[512,512]{1,0:T(8,128)S(1)}, u32[]{:S(2)}, u32[]{:S(2)}) collective-permute-start(f32[512,512]{1,0:T(8,128)S(1)} %get-tuple-element.21), channel_id=1, source_target_pairs={{0,1},{1,0},{2,3},{3,2},{4,5},{5,4},{6,7},{7,6},{8,9},{9,8},{10,11... | collective-permute-start | bytes 3145736 | tf_op jit(solution)/shard_map/ppermute | solution.py:20
  48.3 27.9 %collective-permute-start.4 = (f32[512,512]{1,0:T(8,128)S(1)}, f32[512,512]{1,0:T(8,128)S(1)}, u32[]{:S(2)}, u32[]{:S(2)}) collective-permute-start(f32[512,512]{1,0:T(8,128)S(1)} %get-tuple-element.20), channel_id=1, source_target_pairs={{0,1},{1,0},{2,3},{3,2},{4,5},{5,4},{6,7},{7,6},{8,9},{9,8},{10,11... | collective-permute-start | bytes 3145736 | tf_op jit(solution)/shard_map/ppermute | solution.py:20
  52.1 20.5 %collective-permute-start.12 = (bf16[512,512]{1,0:T(8,128)(2,1)S(1)}, bf16[512,512]{1,0:T(8,128)(2,1)S(1)}, u32[]{:S(2)}, u32[]{:S(2)}) collective-permute-start(bf16[512,512]{1,0:T(8,128)(2,1)S(1)} %get-tuple-element.8), channel_id=1, source_target_pairs={{0,2},{1,3},{2,0},{3,1},{4,6},{5,7},{6,4},{7,5},{8,10},{9,11},{10,... | collective-permute-start | bytes 1572872 | tf_op jit(solution)/shard_map/ppermute | solution.py:20
  73.6 67.1 %collective-permute-start.13 = (f32[512,512]{1,0:T(8,128)}, f32[512,512]{1,0:T(8,128)}, u32[]{:S(2)}, u32[]{:S(2)}) collective-permute-start(f32[512,512]{1,0:T(8,128)} %join.10), channel_id=1, source_target_pairs={{0,4},{1,5},{2,6},{3,7},{4,0},{5,1},{6,2},{7,3},{8,12},{9,13},{10,... | collective-permute-start | bytes 3145736 | tf_op jit(solution)/shard_map/ppermute | solution.py:20
  75.8 4.5 %copy-start.19 = (s32[64]{0:T(128)S(1)}, s32[64]{0:T(128)}, u32[]{:S(2)}) copy-start(s32[64]{0:T(128)} %param.13) | copy-start | bytes 772
  75.8 4.7 %copy-start.20 = (s32[64]{0:T(128)S(1)}, s32[64]{0:T(128)}, u32[]{:S(2)}) copy-start(s32[64]{0:T(128)} %param.14) | copy-start | bytes 772
  75.8 30.1 %collective-permute-start.9 = (bf16[512,512]{1,0:T(8,128)(2,1)}, bf16[512,512]{1,0:T(8,128)(2,1)S(1)}, u32[]{:S(2)}, u32[]{:S(2)}) collective-permute-start(bf16[512,512]{1,0:T(8,128)(2,1)} %get-tuple-element.10), channel_id=1, source_target_pairs={{0,2},{1,3},{2,0},{3,1},{4,6},{5,7},{6,4},{7,5},{8,10},{9,11},{10,... | collective-permute-start | bytes 1572872 | tf_op jit(solution)/shard_map/ppermute | solution.py:20
  78.3 50.2 %collective-permute-start.5 = (bf16[512,512]{1,0:T(8,128)(2,1)}, bf16[512,512]{1,0:T(8,128)(2,1)}, u32[]{:S(2)}, u32[]{:S(2)}) collective-permute-start(bf16[512,512]{1,0:T(8,128)(2,1)} %get-tuple-element.16), channel_id=1, source_target_pairs={{0,2},{1,3},{2,0},{3,1},{4,6},{5,7},{6,4},{7,5},{8,10},{9,11},{10,... | collective-permute-start | bytes 1572872 | tf_op jit(solution)/shard_map/ppermute | solution.py:20
  79.8 59.7 %collective-permute-start.2 = (bf16[512,512]{1,0:T(8,128)(2,1)}, bf16[512,512]{1,0:T(8,128)(2,1)}, u32[]{:S(2)}, u32[]{:S(2)}) collective-permute-start(bf16[512,512]{1,0:T(8,128)(2,1)} %get-tuple-element.18), channel_id=1, source_target_pairs={{0,2},{1,3},{2,0},{3,1},{4,6},{5,7},{6,4},{7,5},{8,10},{9,11},{10,... | collective-permute-start | bytes 1572872 | tf_op jit(solution)/shard_map/ppermute | solution.py:20
  105.9 3.5 %copy-start.1 = (f32[8,512,512]{2,1,0:T(8,128)S(1)}, f32[8,512,512]{2,1,0:T(8,128)}, u32[]{:S(2)}) copy-start(f32[8,512,512]{2,1,0:T(8,128)} %copy-done) | copy-start | bytes 25165828
  109.3 19.1 %copy-start.10 = (f32[512,512]{1,0:T(8,128)S(1)}, f32[512,512]{1,0:T(8,128)}, u32[]{:S(2)}) copy-start(f32[512,512]{1,0:T(8,128)} %get-tuple-element.17.mine_ref) | copy-start | bytes 3145732
  128.4 11.1 %copy-start.9 = (f32[512,512]{1,0:T(8,128)S(1)}, f32[512,512]{1,0:T(8,128)}, u32[]{:S(2)}) copy-start(f32[512,512]{1,0:T(8,128)} %get-tuple-element.19.mine_ref) | copy-start | bytes 3145732
  129.7 11.0 %copy-start.6 = (f32[512,512]{1,0:T(8,128)}, f32[512,512]{1,0:T(8,128)S(1)}, u32[]{:S(2)}) copy-start(f32[512,512]{1,0:T(8,128)S(1)} %join.8.rest_1_) | copy-start | bytes 3145732
  140.7 2.7 %copy-start.11 = (bf16[512,512]{1,0:T(8,128)(2,1)S(1)}, bf16[512,512]{1,0:T(8,128)(2,1)}, u32[]{:S(2)}) copy-start(bf16[512,512]{1,0:T(8,128)(2,1)} %cotangent_ref.1) | copy-start | bytes 1572868
  142.9 27.9 %collective-permute-start.18 = (bf16[512,512]{1,0:T(8,128)(2,1)}, bf16[512,512]{1,0:T(8,128)(2,1)}, u32[]{:S(2)}, u32[]{:S(2)}) collective-permute-start(bf16[512,512]{1,0:T(8,128)(2,1)} %join.11.rest_0_), channel_id=1, source_target_pairs={{0,8},{1,9},{2,10},{3,11},{4,12},{5,13},{6,14},{7,15},{8,0},{9,1},... | collective-permute-start | bytes 1572872 | tf_op jit(solution)/shard_map/ppermute | solution.py:20
  143.4 1.2 copy-start.7
  147.7 1.3 collective-permute-start.14
  149.0 4.3 %collective-permute-start.15 = (f32[32,512]{1,0:T(8,128)S(1)}, f32[32,512]{1,0:T(8,128)S(1)}, u32[]{:S(2)}, u32[]{:S(2)}) collective-permute-start(f32[32,512]{1,0:T(8,128)S(1)} %add.47), channel_id=1, source_target_pairs={{0,2},{1,3},{2,0},{3,1},{4,6},{5,7},{6,4},{7,5},{8,10},{9,11},{10,... | collective-permute-start | bytes 196616 | tf_op jit(solution)/shard_map/ppermute | solution.py:20
  153.4 7.9 %collective-permute-start.16 = (f32[32,512]{1,0:T(8,128)S(1)}, f32[32,512]{1,0:T(8,128)S(1)}, u32[]{:S(2)}, u32[]{:S(2)}) collective-permute-start(f32[32,512]{1,0:T(8,128)S(1)} %add.48), channel_id=1, source_target_pairs={{0,4},{1,5},{2,6},{3,7},{4,0},{5,1},{6,2},{7,3},{8,12},{9,13},{10,... | collective-permute-start | bytes 196616 | tf_op jit(solution)/shard_map/ppermute | solution.py:20
  161.3 9.5 %collective-permute-start.17 = (f32[32,512]{1,0:T(8,128)S(1)}, f32[32,512]{1,0:T(8,128)S(1)}, u32[]{:S(2)}, u32[]{:S(2)}) collective-permute-start(f32[32,512]{1,0:T(8,128)S(1)} %add.49), channel_id=1, source_target_pairs={{0,8},{1,9},{2,10},{3,11},{4,12},{5,13},{6,14},{7,15},{8,0},{9,1},... | collective-permute-start | bytes 196616 | tf_op jit(solution)/shard_map/ppermute | solution.py:20
  171.0 0.8 copy-start.17
  171.1 1.0 copy-start.15
  174.7 4.8 %copy-start.8 = (f32[512,512]{1,0:T(8,128)S(1)}, f32[512,512]{1,0:T(8,128)}, u32[]{:S(2)}) copy-start(f32[512,512]{1,0:T(8,128)} %copy-done.6) | copy-start | bytes 3145732
  174.7 6.4 %copy-start.18 = (bf16[32,16,512]{2,1,0:T(8,128)(2,1)S(1)}, bf16[32,16,512]{2,1,0:T(8,128)(2,1)}, u32[]{:S(2)}) copy-start(bf16[32,16,512]{2,1,0:T(8,128)(2,1)} %copy-done.17) | copy-start | bytes 1572868
  174.7 8.9 %copy-start.16 = (bf16[32,16,512]{2,1,0:T(8,128)(2,1)S(1)}, bf16[32,16,512]{2,1,0:T(8,128)(2,1)}, u32[]{:S(2)}) copy-start(bf16[32,16,512]{2,1,0:T(8,128)(2,1)} %copy-done.15) | copy-start | bytes 1572868
  174.7 73.7 %all-to-all-start.1 = ((bf16[16,32,2304]{2,1,0:T(8,128)(2,1)}), bf16[16,32,2304]{2,1,0:T(8,128)(2,1)}, u32[]{:S(2)}, u32[]{:S(2)}) async-start(bf16[16,32,2304]{2,1,0:T(8,128)(2,1)} %bitcast.22.rest_0_), calls=%async_computation.1 | async-start | bytes 4718592 | tf_op jit(solution)/shard_map/all_to_all | solution.py:288
  179.5 63.3 %collective-permute-start.6 = (f32[512,512]{1,0:T(8,128)S(1)}, f32[512,512]{1,0:T(8,128)}, u32[]{:S(2)}, u32[]{:S(2)}) collective-permute-start(f32[512,512]{1,0:T(8,128)S(1)} %copy-done.8), channel_id=1, source_target_pairs={{0,4},{1,5},{2,6},{3,7},{4,0},{5,1},{6,2},{7,3},{8,12},{9,13},{10,... | collective-permute-start | bytes 3145736 | tf_op jit(solution)/shard_map/ppermute | solution.py:20
  187.5 3.4 %copy-start.5 = (bf16[8192,512]{1,0:T(8,128)(2,1)S(1)}, bf16[8192,512]{1,0:T(8,128)(2,1)}, u32[]{:S(2)}) copy-start(bf16[8192,512]{1,0:T(8,128)(2,1)} %all-gather.3.cloned.1.call-done) | copy-start | bytes 25165828
  190.9 1.5 copy-start.12
  242.8 1.5 copy-start.2
  244.3 1.8 copy-start.3
  246.1 1.4 copy-start.13
Sparse Core Ops, SparseCore 0:
  10.2 135.5 all-gather.2
